TPU v7x, 32 devices: a whole 2x2x4 slice. The times are simulated.
32 devices in a mesh: dp: 16 (over z, x, core), tensor: 2 (over y).
Axes of the slice: x: 2, y: 2, z: 4, core: 2. Of those that a mesh axis runs over, the one named last changes fastest.
Arguments:
- hidden: bfloat16 [32, 1024, 1024], P('dp'), may hold values from -6 to 6
- segment_ids: int32 [32, 1024], P('dp'), may hold values from 0 to 3, never falling along the last dimension, each value on 1 to 800 neighbouring positions
- norm_gain: float32 [1024], replicated, may hold values from 0.1 to 1.9
- proj_gate: bfloat16 [1024, 2048], P(None, 'tensor'), may hold values from -0.1875 to 0.1875
- proj_value: bfloat16 [1024, 2048], P(None, 'tensor'), may hold values from -0.1875 to 0.1875
- proj_state: bfloat16 [1024, 256], replicated, may hold values from -0.1875 to 0.1875
- proj_step: bfloat16 [1024, 32], P(None, 'tensor'), may hold values from -0.1875 to 0.1875
- conv_value: float32 [4, 2048], P(None, 'tensor'), may hold values from -3 to 3
- conv_value_bias: float32 [2048], P('tensor'), may hold values from -3 to 3
- conv_state: float32 [4, 256], replicated, may hold values from -3 to 3
- conv_state_bias: float32 [256], replicated, may hold values from -3 to 3
- step_bias: float32 [32], P('tensor'), may hold values from -6 to -2
- decay_log: float32 [32], P('tensor'), may hold values from 0 to 2.77
- skip_gain: float32 [32], P('tensor'), may hold values from 0.5 to 1.5
- gate_gain: float32 [2048], P('tensor'), may hold values from 0.1 to 1.9
- proj_out: bfloat16 [1024, 2048], P(None, 'tensor'), may hold values from -0.125 to 0.125
- out_grad: bfloat16 [32, 1024, 1024], P('dp'), may hold values from -6 to 6
Outputs:
- block_out: bfloat16 [32, 1024, 1024], P('dp')
- grad_hidden: float32 [32, 1024, 1024], P('dp')
- grad_norm_gain: float32 [1024], replicated
- grad_proj_gate: float32 [1024, 2048], P('dp', 'tensor')
- grad_proj_value: float32 [1024, 2048], P('dp', 'tensor')
- grad_proj_state: float32 [1024, 256], P('dp')
- grad_proj_step: float32 [1024, 32], P('dp', 'tensor')
- grad_conv_value: float32 [4, 2048], P(None, 'tensor')
- grad_conv_value_bias: float32 [2048], P('tensor')
- grad_conv_state: float32 [4, 256], replicated
- grad_conv_state_bias: float32 [256], replicated
- grad_step_bias: float32 [32], P('tensor')
- grad_decay_log: float32 [32], P('tensor')
- grad_skip_gain: float32 [32], P('tensor')
- grad_gate_gain: float32 [2048], P('tensor')
- grad_proj_out: float32 [1024, 2048], P('dp', 'tensor')
Inputs may be any that keep to these rules, and one draw needn't show every extreme that they name: `segment_ids`: tokens of a sequence with the same number form one document; numbers never fall along a sequence; each sequence holds 4 documents of 1 to 800 tokens, one of exactly 800.
All inputs are finite; a program needn't handle non-finite values.
Results may differ from a plain program's by a relative error of at most 0.019.
Values sent between devices are 32-bit elements; how exact they have to be, the bound alone decides.
A program may use at most 192 MiB of HBM per device.

v0:
```python
import jax
import jax.numpy as jnp
from jax import lax
from jax.sharding import PartitionSpec as P

HEAD_DIM = 64
STATE = 128
KERNEL = 4


epsilon = 1e-05
precise = lax.Precision.HIGHEST


def lag_masks(segment_row):
    length = segment_row.shape[0]
    result = [jnp.ones((length,), jnp.float32)]
    for delay in range(1, KERNEL):
        earlier = jnp.concatenate(
            [jnp.full((delay,), -1, jnp.int32), segment_row[: length - delay]]
        )
        result.append((earlier == segment_row).astype(jnp.float32))
    return result


def causal_conv(values, weight, conv_bias, doc_masks):
    length = values.shape[0]
    summed = conv_bias[None, :] + weight[KERNEL - 1][None, :] * values
    for delay in range(1, KERNEL):
        earlier = jnp.concatenate(
            [jnp.zeros((delay, values.shape[1]), jnp.float32), values[: length - delay]], axis=0
        )
        summed = summed + weight[KERNEL - 1 - delay][None, :] * earlier * doc_masks[delay][:, None]
    return jax.nn.silu(summed)


def head_mix(values, states, step_raw, segment_row, step_bias, decay_log, skip_gain):
    length = values.shape[0]
    head_count = step_raw.shape[1]
    state_low = states.astype(jnp.bfloat16)
    value_low = values.astype(jnp.bfloat16)
    state_in = state_low[:, :STATE]
    state_out = state_low[:, STATE:]
    step_size = jax.nn.softplus(step_raw + step_bias[None, :])
    decay_rate = -jnp.exp(decay_log)
    running = jnp.cumsum(step_size * decay_rate[None, :], axis=0).T
    places = jnp.arange(length)
    allowed = (places[:, None] >= places[None, :]) & (segment_row[:, None] == segment_row[None, :])
    affinity = lax.dot_general(
        state_out, state_in, (((1,), (1,)), ((), ())), preferred_element_type=jnp.float32
    )
    decays = jnp.exp(jnp.where(allowed[None], running[:, :, None] - running[:, None, :], -1e30))
    mixing = (decays * affinity[None] * step_size.T[:, None, :]).astype(jnp.bfloat16)
    per_head = values.reshape(length, head_count, HEAD_DIM)
    low_head = value_low.reshape(length, head_count, HEAD_DIM)
    mixed_out = jnp.einsum("hts,shp->thp", mixing, low_head, preferred_element_type=jnp.float32)
    mixed_out = mixed_out + skip_gain[None, :, None] * per_head
    return mixed_out.reshape(length, head_count * HEAD_DIM)


def mixer_all(
    value_raw,
    state_raw,
    step_raw,
    segment_ids,
    conv_value,
    conv_value_bias,
    conv_state,
    conv_state_bias,
    step_bias,
    decay_log,
    skip_gain,
):

    def per_sequence(items):
        value_row, state_row, step_row, segment_row = items
        doc_masks = lag_masks(segment_row)
        value_conv = causal_conv(value_row, conv_value, conv_value_bias, doc_masks)
        state_conv = causal_conv(state_row, conv_state, conv_state_bias, doc_masks)
        return head_mix(
            value_conv, state_conv, step_row, segment_row, step_bias, decay_log, skip_gain
        )

    return lax.map(jax.checkpoint(per_sequence), (value_raw, state_raw, step_raw, segment_ids))


def right_product(left, weight):
    return lax.dot_general(
        left, weight, (((1,), (1,)), ((), ())), preferred_element_type=jnp.float32
    )


def right_precise(left, weight):
    return lax.dot_general(
        left,
        weight,
        (((1,), (1,)), ((), ())),
        precision=precise,
        preferred_element_type=jnp.float32,
    )


def token_product(left, right):
    return lax.dot_general(
        left, right, (((0,), (0,)), ((), ())), preferred_element_type=jnp.float32
    )


def token_precise(left, right):
    return lax.dot_general(
        left, right, (((0,), (0,)), ((), ())), precision=precise, preferred_element_type=jnp.float32
    )


def local(
    hidden,
    segment_ids,
    norm_gain,
    proj_gate,
    proj_value,
    proj_state,
    proj_step,
    conv_value,
    conv_value_bias,
    conv_state,
    conv_state_bias,
    step_bias,
    decay_log,
    skip_gain,
    gate_gain,
    proj_out,
    out_grad,
):
    seq_count, length, width = hidden.shape
    local_inner = proj_gate.shape[1]
    local_heads = proj_step.shape[1]
    state_width = proj_state.shape[1]
    tensor_count = lax.axis_size("tensor")
    inner_total = local_inner * tensor_count
    token_rows = seq_count * length
    wide = hidden.astype(jnp.float32).reshape(token_rows, width)
    row_scale = lax.rsqrt(jnp.mean(wide * wide, axis=-1, keepdims=True) + epsilon)
    normed = (wide * row_scale * norm_gain[None, :]).astype(jnp.bfloat16)
    gate_raw = jnp.dot(normed, proj_gate, preferred_element_type=jnp.float32)
    value_raw = jnp.dot(normed, proj_value, preferred_element_type=jnp.float32)
    state_raw = jnp.dot(normed, proj_state, preferred_element_type=jnp.float32)
    step_raw = jnp.dot(normed, proj_step, preferred_element_type=jnp.float32)

    def mixer(
        value_in,
        state_in,
        step_in,
        cv_weight,
        cv_bias,
        cs_weight,
        cs_bias,
        sb_param,
        dl_param,
        sg_param,
    ):
        mixed_seq = mixer_all(
            value_in.reshape(seq_count, length, local_inner),
            state_in.reshape(seq_count, length, state_width),
            step_in.reshape(seq_count, length, local_heads),
            segment_ids,
            cv_weight,
            cv_bias,
            cs_weight,
            cs_bias,
            sb_param,
            dl_param,
            sg_param,
        )
        return mixed_seq.reshape(token_rows, local_inner)

    mixed_out, mixer_back = jax.vjp(
        mixer,
        value_raw,
        state_raw,
        step_raw,
        conv_value,
        conv_value_bias,
        conv_state,
        conv_state_bias,
        step_bias,
        decay_log,
        skip_gain,
    )
    gate_act = jax.nn.silu(gate_raw)
    gated = mixed_out * gate_act
    squares = lax.psum(jnp.sum(gated * gated, axis=-1), "tensor")
    gated_scale = lax.rsqrt(squares / inner_total + epsilon)[:, None]
    output_in = (gated * gated_scale * gate_gain[None, :]).astype(jnp.bfloat16)
    branch = lax.psum(right_product(output_in, proj_out), "tensor")
    block_out = (wide + branch).astype(jnp.bfloat16).reshape(seq_count, length, width)
    cotangent = out_grad.reshape(token_rows, width)
    cot_wide = cotangent.astype(jnp.float32)
    d_output_in = jnp.dot(cotangent, proj_out, preferred_element_type=jnp.float32)
    grad_gate_gain = jnp.sum(d_output_in * gated * gated_scale, axis=0)
    weighted = d_output_in * gate_gain[None, :]
    gate_inner = lax.psum(jnp.sum(weighted * gated, axis=-1), "tensor")
    d_gated = gated_scale * weighted - gated_scale**3 * gated * gate_inner[:, None] / inner_total
    sigma = jax.nn.sigmoid(gate_raw)
    d_mixed = d_gated * gate_act
    d_gate = (d_gated * mixed_out * sigma * (1.0 + gate_raw * (1.0 - sigma))).astype(jnp.bfloat16)
    (
        d_value_wide,
        d_state_part,
        d_step_wide,
        g_conv_value,
        g_conv_value_bias,
        g_conv_state,
        g_conv_state_bias,
        g_step_bias,
        g_decay,
        g_skip,
    ) = mixer_back(d_mixed)
    d_value = d_value_wide.astype(jnp.bfloat16)
    d_step = d_step_wide.astype(jnp.bfloat16)
    d_normed_part = (
        right_product(d_gate, proj_gate)
        + right_product(d_value, proj_value)
        + right_product(d_step, proj_step)
    )
    state_wide = proj_state.astype(jnp.float32)
    d_normed_sum, d_state = lax.psum((d_normed_part, d_state_part), "tensor")
    d_normed = d_normed_sum + right_precise(d_state, state_wide)
    d_scaled = d_normed * norm_gain[None, :]
    norm_inner = jnp.sum(d_scaled * wide, axis=-1, keepdims=True)
    grad_wide = cot_wide + row_scale * d_scaled - row_scale**3 * wide * norm_inner / width
    grad_norm_gain = jnp.sum(d_normed * wide * row_scale, axis=0)
    grad_hidden = grad_wide.reshape(seq_count, length, width)
    inner_grads = jnp.concatenate([d_gate, d_value], axis=1)
    state_term = token_precise(normed.astype(jnp.float32), d_state)
    weight_rows = lax.psum_scatter(
        jnp.concatenate(
            [
                token_product(normed, inner_grads),
                state_term,
                token_product(normed, d_step),
                token_product(cotangent, output_in),
            ],
            axis=1,
        ),
        "dp",
        scatter_dimension=0,
        tiled=True,
    )
    edge_value = 2 * local_inner
    edge_state = edge_value + state_width
    edge_step = edge_state + local_heads
    grad_proj_gate = weight_rows[:, :local_inner]
    grad_proj_value = weight_rows[:, local_inner:edge_value]
    grad_proj_state = weight_rows[:, edge_value:edge_state]
    grad_proj_step = weight_rows[:, edge_state:edge_step]
    grad_proj_out = weight_rows[:, edge_step:]
    (
        grad_conv_value,
        grad_conv_value_bias,
        grad_step_bias,
        grad_decay_log,
        grad_skip_gain,
        grad_gate_gain,
        grad_norm_gain,
    ) = lax.psum(
        (
            g_conv_value,
            g_conv_value_bias,
            g_step_bias,
            g_decay,
            g_skip,
            grad_gate_gain,
            grad_norm_gain,
        ),
        "dp",
    )
    grad_conv_state, grad_conv_state_bias = lax.psum(
        (g_conv_state, g_conv_state_bias), ("dp", "tensor")
    )
    return (
        block_out,
        grad_hidden,
        grad_norm_gain,
        grad_proj_gate,
        grad_proj_value,
        grad_proj_state,
        grad_proj_step,
        grad_conv_value,
        grad_conv_value_bias,
        grad_conv_state,
        grad_conv_state_bias,
        grad_step_bias,
        grad_decay_log,
        grad_skip_gain,
        grad_gate_gain,
        grad_proj_out,
    )


def solution(mesh):
    in_specs = (
        P("dp", None, None),
        P("dp", None),
        P(),
        P(None, "tensor"),
        P(None, "tensor"),
        P(),
        P(None, "tensor"),
        P(None, "tensor"),
        P("tensor"),
        P(),
        P(),
        P("tensor"),
        P("tensor"),
        P("tensor"),
        P("tensor"),
        P(None, "tensor"),
        P("dp", None, None),
    )
    out_specs = (
        P("dp", None, None),
        P("dp", None, None),
        P(),
        P("dp", "tensor"),
        P("dp", "tensor"),
        P("dp", None),
        P("dp", "tensor"),
        P(None, "tensor"),
        P("tensor"),
        P(),
        P(),
        P("tensor"),
        P("tensor"),
        P("tensor"),
        P("tensor"),
        P("dp", "tensor"),
    )
    return jax.shard_map(local, mesh=mesh, in_specs=in_specs, out_specs=out_specs, check_vma=False)
```

profile of v0, /device:TPU:0, one launch (start us, length us, event | category | flops | bytes accessed | tf_op | source)
XLA Modules:
  0.0 1168.9 jit_solution(6771093158376481078)
XLA Ops:
  11.2 8.8 fusion.80
  25.0 109.6 %while.45 = (s32[]{:T(128)}, f32[2,1024,1024]{2,1,0:T(8,128)}, f32[1,1024]{1,0:T(1,128)S(1)}, f32[1,1024]{1,0:T(1,128)S(1)}, f32[2,1024,1024]{1,2,0:T(8,128)}, /...) while((s32[]{:T(128)}, f32[2,1024,1024]{2,1,0:T(8,128)}, ...), condition=%wide.region_4.5_spmd.clone, body=%wide.region_1.4_spmd.clone.sunk | while | flops 2528256000 | bytes 140342752 | solution.py:84
  47.9 21.9 %bitcast_add_fusion.5 = f32[1024,16,64]{0,2,1:T(8,128)} fusion(f32[1024,16,64]{0,2,1:T(8,128)} %bitcast.459, bf16[1024,16,64]{0,2,1:T(8,128)(2,1)} %bitcast.462, f32[16,1024]{1,0:T(8,128)S(1)} %get-tuple-element.1440, f32[1024,1024]{1,0:T(8,128)} %fusion.160, f32[16,1024]{1,0:T(8,128)S(1)} %bitcast.488, pred[1024,1024]{1,0:T(8,128)(4,1)S(1)} %fusion.161, ...), kind=kOutput, calls=%fused_computation.7.clone.1 | convolution fusion | flops 2233466880 | bytes 15859776 | tf_op jit(solution)/shard_map/jvp()/while/body/eval_jaxpr/hts,shp->thp/dot_general | solution.py:56
  102.6 21.9 %bitcast_add_fusion.5 = f32[1024,16,64]{0,2,1:T(8,128)} fusion(f32[1024,16,64]{0,2,1:T(8,128)} %bitcast.459, bf16[1024,16,64]{0,2,1:T(8,128)(2,1)} %bitcast.462, f32[16,1024]{1,0:T(8,128)S(1)} %get-tuple-element.1440, f32[1024,1024]{1,0:T(8,128)} %fusion.160, f32[16,1024]{1,0:T(8,128)S(1)} %bitcast.488, pred[1024,1024]{1,0:T(8,128)(4,1)S(1)} %fusion.161, ...), kind=kOutput, calls=%fused_computation.7.clone.1 | convolution fusion | flops 2233466880 | bytes 15859776 | tf_op jit(solution)/shard_map/jvp()/while/body/eval_jaxpr/hts,shp->thp/dot_general | solution.py:56
  140.8 10.0 multiply_reduce_fusion.11
  156.7 11.9 %fusion.93 = f32[2048,1024]{1,0:T(8,128)} fusion(bf16[1024,1024]{1,0:T(8,128)(2,1)} %param.36, f32[2048,1024]{1,0:T(8,128)} %get-tuple-element.1089, f32[1024]{0:T(1024)S(1)} %copy-done.87, f32[2048]{0:T(1024)S(1)} %get-tuple-element.1131), kind=kOutput, calls=%fused_computation.208 | convolution fusion | flops 4301258752 | bytes 18886656 | tf_op jit(solution)/shard_map/dot_general | solution.py:88
  181.5 18.6 %fusion.79 = (f32[2048,1024]{1,0:T(8,128)}, bf16[2048,1024]{1,0:T(8,128)(2,1)}) fusion(f32[2048]{0:T(1024)S(1)} %psum.100, f32[2048,1024]{1,0:T(8,128)} %get-tuple-element.1089, f32[2048,1024]{1,0:T(8,128)} %get-tuple-element.1139, f32[2048]{0:T(1024)S(1)} %get-tuple-element.1130, f32[1024]{0:T(1024)S(1)} %copy-done.87, f32[2048]{0:T(1024)S(1)} %get-tuple-element.1131, ...), kind=kLoop, calls=%fused_computation.189 | loop fusion | flops 37748736 | bytes 46166016 | tf_op jit(solution)/shard_map/mul | solution.py:204
  204.7 332.0 %while.46 = (s32[]{:T(128)}, f32[1024]{0:T(1024)}, f32[4,1024]{1,0:T(4,128)}, f32[256]{0:T(256)}, f32[4,256]{1,0:T(4,128)}, /*index=5*/f32[16]{0:T(128)}, f32[16...) while((s32[]{:T(128)}, f32[1024]{0:T(1024)}, ...), condition=%wide.region_33.34_spmd.clone, body=%wide.region_10.33_spmd.clone.sunk | while | flops 5490891776 | bytes 369435104 | solution.py:84
  233.3 23.4 %convert_convert_fusion.2 = f32[16,64,1024]{2,1,0:T(8,128)} fusion(f32[16,64,1024]{2,1,0:T(8,128)} %bitcast.455, f32[16,1024]{1,0:T(8,128)S(1)} %get-tuple-element.1481, f32[1024,1024]{1,0:T(8,128)} %fusion.174, f32[16,1024]{1,0:T(8,128)S(1)} %bitcast.486, pred[1024,1024]{1,0:T(8,128)(4,1)} %fusion.175), kind=kOutput, calls=%fused_computation.84.clone.1 | convolution fusion | flops 2232418304 | bytes 13762560 | tf_op jit(solution)/shard_map/transpose(jvp())/while/body/eval_jaxpr/checkpoint/hts,shp->thp/dot_general | solution.py:56
  265.3 8.7 multiply_reduce_fusion.18
  274.0 50.9 %fusion.176 = (f32[16,1024]{1,0:T(8,128)S(1)}, f32[16,1024]{1,0:T(8,128)S(1)}, f32[16,1024]{1,0:T(8,128)S(1)}, bf16[1024,1024]{1,0:T(8,128)(2,1)S(1)}) fusion(f32[16,1024]{1,0:T(8,128)S(1)} %get-tuple-element.1481, f32[1024,1024]{1,0:T(8,128)S(1)} %copy-done.9, f32[16,1024]{1,0:T(8,128)S(1)} %bitcast.487, pred[1024,1024]{1,0:T(8,128)(4,1)S(1)} %copy-done.16, ...), kind=kOutput, calls=%fused_computation.58.clone.1 | convolution fusion | flops 2381266944 | bytes 13959168 | tf_op jit(solution)/shard_map/transpose(jvp())/while/body/eval_jaxpr/checkpoint/hts,shp->thp/dot_general | solution.py:56
  343.7 19.8 %reduce-window.74 = f32[16,8,128]{2,1,0:T(8,128)S(1)} reduce-window(f32[16,8,128]{2,1,0:T(8,128)S(1)} %bitcast.473, f32[]{:T(128)} %constant.197.clone.1..sunk.1), window={size=1x1x128 pad=0_0x0_0x0_127}, to_apply=%region_27.27 | reduce-window | flops 2080768 | bytes 131076 | tf_op jit(solution)/shard_map/reduce-window.32
  395.7 23.4 %convert_convert_fusion.2 = f32[16,64,1024]{2,1,0:T(8,128)} fusion(f32[16,64,1024]{2,1,0:T(8,128)} %bitcast.455, f32[16,1024]{1,0:T(8,128)S(1)} %get-tuple-element.1481, f32[1024,1024]{1,0:T(8,128)} %fusion.174, f32[16,1024]{1,0:T(8,128)S(1)} %bitcast.486, pred[1024,1024]{1,0:T(8,128)(4,1)} %fusion.175), kind=kOutput, calls=%fused_computation.84.clone.1 | convolution fusion | flops 2232418304 | bytes 13762560 | tf_op jit(solution)/shard_map/transpose(jvp())/while/body/eval_jaxpr/checkpoint/hts,shp->thp/dot_general | solution.py:56
  436.4 50.9 %fusion.176 = (f32[16,1024]{1,0:T(8,128)S(1)}, f32[16,1024]{1,0:T(8,128)S(1)}, f32[16,1024]{1,0:T(8,128)S(1)}, bf16[1024,1024]{1,0:T(8,128)(2,1)S(1)}) fusion(f32[16,1024]{1,0:T(8,128)S(1)} %get-tuple-element.1481, f32[1024,1024]{1,0:T(8,128)S(1)} %copy-done.9, f32[16,1024]{1,0:T(8,128)S(1)} %bitcast.487, pred[1024,1024]{1,0:T(8,128)(4,1)S(1)} %copy-done.16, ...), kind=kOutput, calls=%fused_computation.58.clone.1 | convolution fusion | flops 2381266944 | bytes 13959168 | tf_op jit(solution)/shard_map/transpose(jvp())/while/body/eval_jaxpr/checkpoint/hts,shp->thp/dot_general | solution.py:56
  506.1 19.8 %reduce-window.74 = f32[16,8,128]{2,1,0:T(8,128)S(1)} reduce-window(f32[16,8,128]{2,1,0:T(8,128)S(1)} %bitcast.473, f32[]{:T(128)} %constant.197.clone.1..sunk.1), window={size=1x1x128 pad=0_0x0_0x0_127}, to_apply=%region_27.27 | reduce-window | flops 2080768 | bytes 131076 | tf_op jit(solution)/shard_map/reduce-window.32
  565.3 11.3 convolution_bitcast_fusion
  576.7 11.3 fusion.59
  588.0 398.5 %all-reduce.37.cloned.1.call-done = (f32[2048,1024]{1,0:T(8,128)}, f32[2048,1024]{1,0:T(8,128)}, f32[2048,256]{1,0:T(8,128)}) async-done(((f32[2048,1024]{1,0:T(8,128)}, f32[2048,1024]{1,0:T(8,128)}, f32[2048,256]{1,0:T(8,128)}), (f32[2048,1024]{1,0:T(8,128)}, f32[2048,1024]{1,0:T(8,128)}, f32[2048,256]{1,0:T(8,128)})) %all-reduce.37.cloned.1.call-update) | async-done | bytes 18874384 | tf_op jit(solution)/shard_map/psum | solution.py:194
  993.8 15.5 %concatenate.75 = f32[1024,3344]{1,0:T(8,128)} concatenate(f32[1024,2048]{1,0:T(8,128)} %fusion.59, f32[1024,256]{1,0:T(8,128)S(1)} %fusion.105, f32[1024,16]{1,0:T(8,128)} %convolution_bitcast_fusion.1, f32[1024,1024]{1,0:T(8,128)} %convolution_bitcast_fusion), dimensions={1} | concatenate | bytes 27394048 | tf_op jit(solution)/shard_map/concatenate | solution.py:236
  1010.0 40.7 %all-reduce.32 = (f32[4,256]{1,0:T(4,128)}, f32[256]{0:T(256)}) all-reduce(f32[4,256]{1,0:T(4,128)S(1)} %copy-done.50, f32[256]{0:T(256)S(1)} %copy-done.71), channel_id=1, replica_groups=mesh['dp'=16,'tensor'=2] {'dp','tensor'}, use_global_device_ids=true, to_apply=%region_42.43 | all-reduce | flops 1280 | bytes 10240 | tf_op jit(solution)/shard_map/psum | solution.py:277
  1050.8 11.3 fusion.77
  1062.2 63.5 %all-reduce.33 = (f32[1024]{0:T(1024)}, f32[4,1024]{1,0:T(4,128)}, f32[1024]{0:T(1024)}, f32[16]{0:T(128)}, f32[16]{0:T(128)}, /*index=5*/f32[16]{0:T(128)}, f32[1024]{0:T(1024)}) all-reduce(f32[1024]{0:T(1024)S(1)} %get-tuple-element.968, f32[4,1024]{1,0:T(4,128)S(1)} %copy-done.37, ...), channel_id=1, replica_groups=mesh['dp'=16,'tensor'=2] {'dp'}, use_global_device_ids=true, to_apply=%region_38.39 | all-reduce | flops 7216 | bytes 57728 | tf_op jit(solution)/shard_map/psum | solution.py:265
  1125.7 14.8 %fusion.74 = (f32[2048,1024]{1,0:T(8,128)}, bf16[2048,1024]{1,0:T(8,128)(2,1)}) fusion(bf16[2,1024,1024]{2,1,0:T(8,128)(2,1)} %param.21, f32[2048,1024]{1,0:T(8,128)} %get-tuple-element.1140, f32[2048]{0:T(1024)S(1)} %get-tuple-element.969, f32[2048]{0:T(1024)S(1)} %multiply_multiply_fusion, f32[1024]{0:T(1024)S(1)} %copy-done.68, f32[2048]{0:T(1024)S(1)} %bitcast.526, ...), kind=kLoop, calls=%fused_computation.176 | loop fusion | flops 23068672 | bytes 37777408 | tf_op jit(solution)/shard_map/sub | solution.py:230
  1140.5 16.3 %reduce-scatter.2.cloned.1.call-done = f32[64,3344]{1,0:T(8,128)} async-done(((f32[1024,3344]{1,0:T(8,128)}), f32[64,3344]{1,0:T(8,128)}) %reduce-scatter.2.cloned.1.call-update) | async-done | bytes 856080 | tf_op jit(solution)/shard_map/reduce_scatter | solution.py:235
  (483 shorter events, 271.7 us)
Async XLA Ops:
  7.2 130.4 %copy-start = (bf16[1024,1024]{1,0:T(8,128)(2,1)S(1)}, bf16[1024,1024]{1,0:T(8,128)(2,1)}, u32[]{:S(2)}) copy-start(bf16[1024,1024]{1,0:T(8,128)(2,1)} %param.24) | copy-start | bytes 6291460
  7.2 979.3 %all-reduce.37.cloned.1.call-start = ((), (), s32[]{:S(2)}) async-start(), calls=%async_computation.2 | async-start | bytes 37748736 | tf_op jit(solution)/shard_map/psum | solution.py:194
  25.0 109.6 %copy-start.62 = (f32[1,8,2,128]{3,2,1,0:T(2,128)S(1)}, f32[1,8,2,128]{3,2,1,0:T(2,128)}, u32[]{:S(2)}) copy-start(f32[1,8,2,128]{3,2,1,0:T(2,128)} %get-tuple-element.1133) | copy-start | bytes 24580
  25.0 109.6 %copy-start.67 = (f32[1024]{0:T(1024)S(1)}, f32[1024]{0:T(1024)}, u32[]{:S(2)}) copy-start(f32[1024]{0:T(1024)} %param.23) | copy-start | bytes 12292
  274.0 50.9 %copy-start.13 = (bf16[1024,256]{1,0:T(8,128)(2,1)S(1)}, bf16[1024,256]{1,0:T(8,128)(2,1)}, u32[]{:S(2)}) copy-start(bf16[1024,256]{1,0:T(8,128)(2,1)} %copy-done.12) | copy-start | bytes 1572868 | tf_op jit(solution)/shard_map/transpose(jvp())/while
  340.4 26.2 %copy-start.54 = (f32[1024]{0:T(1024)S(1)}, f32[1024]{0:T(1024)}, u32[]{:S(2)}) copy-start(f32[1024]{0:T(1024)} %get-tuple-element.1615) | copy-start | bytes 12292 | tf_op jit(solution)/shard_map/transpose(jvp())/while
  340.4 26.4 %copy-start.76 = (f32[16]{0:T(128)S(1)}, f32[16]{0:T(128)}, u32[]{:S(2)}) copy-start(f32[16]{0:T(128)} %get-tuple-element.1621) | copy-start | bytes 196 | tf_op jit(solution)/shard_map/transpose(jvp())/while
  340.4 26.9 %copy-start.31 = (f32[2,1024,16]{1,2,0:T(8,128)S(1)}, f32[2,1024,16]{1,2,0:T(8,128)}, u32[]{:S(2)}) copy-start(f32[2,1024,16]{1,2,0:T(8,128)} %copy-done.30) | copy-start | bytes 393220 | tf_op jit(solution)/shard_map/transpose(jvp())/while
  340.4 26.9 %copy-start.34 = (s32[2,1024]{1,0:T(2,128)S(1)}, s32[2,1024]{1,0:T(2,128)}, u32[]{:S(2)}) copy-start(s32[2,1024]{1,0:T(2,128)} %copy-done.33) | copy-start | bytes 24580 | tf_op jit(solution)/shard_map/transpose(jvp())/while
  340.4 26.9 %copy-start.44 = (f32[1024]{0:T(1024)S(1)}, f32[1024]{0:T(1024)}, u32[]{:S(2)}) copy-start(f32[1024]{0:T(1024)} %copy-done.43) | copy-start | bytes 12292 | tf_op jit(solution)/shard_map/transpose(jvp())/while
  340.4 26.9 %copy-start.53 = (f32[4,256]{1,0:T(4,128)S(1)}, f32[4,256]{1,0:T(4,128)}, u32[]{:S(2)}) copy-start(f32[4,256]{1,0:T(4,128)} %get-tuple-element.1718) | copy-start | bytes 12292 | tf_op jit(solution)/shard_map/transpose(jvp())/while
  340.4 26.9 %copy-start.61 = (f32[256]{0:T(256)S(1)}, f32[256]{0:T(256)}, u32[]{:S(2)}) copy-start(f32[256]{0:T(256)} %copy-done.60) | copy-start | bytes 3076 | tf_op jit(solution)/shard_map/transpose(jvp())/while
  436.4 50.9 %copy-start.13 = (bf16[1024,256]{1,0:T(8,128)(2,1)S(1)}, bf16[1024,256]{1,0:T(8,128)(2,1)}, u32[]{:S(2)}) copy-start(bf16[1024,256]{1,0:T(8,128)(2,1)} %copy-done.12) | copy-start | bytes 1572868 | tf_op jit(solution)/shard_map/transpose(jvp())/while
  502.7 26.2 %copy-start.54 = (f32[1024]{0:T(1024)S(1)}, f32[1024]{0:T(1024)}, u32[]{:S(2)}) copy-start(f32[1024]{0:T(1024)} %get-tuple-element.1615) | copy-start | bytes 12292 | tf_op jit(solution)/shard_map/transpose(jvp())/while
  502.8 26.4 %copy-start.76 = (f32[16]{0:T(128)S(1)}, f32[16]{0:T(128)}, u32[]{:S(2)}) copy-start(f32[16]{0:T(128)} %get-tuple-element.1621) | copy-start | bytes 196 | tf_op jit(solution)/shard_map/transpose(jvp())/while
  502.8 26.9 %copy-start.31 = (f32[2,1024,16]{1,2,0:T(8,128)S(1)}, f32[2,1024,16]{1,2,0:T(8,128)}, u32[]{:S(2)}) copy-start(f32[2,1024,16]{1,2,0:T(8,128)} %copy-done.30) | copy-start | bytes 393220 | tf_op jit(solution)/shard_map/transpose(jvp())/while
  502.8 26.9 %copy-start.34 = (s32[2,1024]{1,0:T(2,128)S(1)}, s32[2,1024]{1,0:T(2,128)}, u32[]{:S(2)}) copy-start(s32[2,1024]{1,0:T(2,128)} %copy-done.33) | copy-start | bytes 24580 | tf_op jit(solution)/shard_map/transpose(jvp())/while
  502.8 26.9 %copy-start.44 = (f32[1024]{0:T(1024)S(1)}, f32[1024]{0:T(1024)}, u32[]{:S(2)}) copy-start(f32[1024]{0:T(1024)} %copy-done.43) | copy-start | bytes 12292 | tf_op jit(solution)/shard_map/transpose(jvp())/while
  502.8 26.9 %copy-start.53 = (f32[4,256]{1,0:T(4,128)S(1)}, f32[4,256]{1,0:T(4,128)}, u32[]{:S(2)}) copy-start(f32[4,256]{1,0:T(4,128)} %get-tuple-element.1718) | copy-start | bytes 12292 | tf_op jit(solution)/shard_map/transpose(jvp())/while
  502.8 26.9 %copy-start.61 = (f32[256]{0:T(256)S(1)}, f32[256]{0:T(256)}, u32[]{:S(2)}) copy-start(f32[256]{0:T(256)} %copy-done.60) | copy-start | bytes 3076 | tf_op jit(solution)/shard_map/transpose(jvp())/while
  559.7 597.1 %reduce-scatter.2.cloned.1.call-start = ((), (), s32[]{:S(2)}) async-start(), calls=%async_computation.1 | async-start | bytes 15040512 | tf_op jit(solution)/shard_map/reduce_scatter | solution.py:235
  1009.3 41.4 %copy-start.63 = (f32[1,8,2,128]{3,2,1,0:T(2,128)S(1)}, f32[1,8,2,128]{3,2,1,0:T(2,128)}, u32[]{:S(2)}) copy-start(f32[1,8,2,128]{3,2,1,0:T(2,128)} %get-tuple-element.1133) | copy-start | bytes 24580
  1009.3 41.4 %copy-start.41 = (bf16[1024,256]{1,0:T(8,128)(2,1)S(1)}, bf16[1024,256]{1,0:T(8,128)(2,1)}, u32[]{:S(2)}) copy-start(bf16[1024,256]{1,0:T(8,128)(2,1)} %param.26) | copy-start | bytes 1572868
  1009.4 41.4 %copy-start.58 = (f32[1,8,2,128]{3,1,2,0:T(8,128)S(1)}, f32[1,8,2,128]{3,1,2,0:T(8,128)}, u32[]{:S(2)}) copy-start(f32[1,8,2,128]{3,1,2,0:T(8,128)} %copy-done.57) | copy-start | bytes 24580
  (115 other events, 1017.6 us)
Sparse Core Ops, SparseCore 0:
  559.8 426.6 all-reduce.36
  1009.5 147.2 reduce-scatter.1
where the time goes:
time: 1180 us; the launch traced here: 1170 us
  waiting for transfers between devices  415 us (35%)
  matrix products  311 us (26%)
  other arithmetic  189 us (16%)
  local copies, waits for them, and re-layouts  115 us (10%)
  blocking collectives  115 us (10%)
  between operations  14.8 us (1%)
    psum x1, waiting for transfers between devices, local(): branch = lax.psum(right_product(output_in, proj_out), 'tensor')  398 us
    dot_general x6, matrix products, head_mix(): jnp.einsum('hts,shp->thp', mixing, low_head, preferred_element_type=jnp.f...  192 us
    psum x1, blocking collectives, local(): lax.psum((g_conv_value, g_conv_value_bias, g_step_bias, g_decay, g_skip,...  63.5 us
    another operation x19, other arithmetic  58.4 us
    psum x1, blocking collectives, local(): lax.psum((g_conv_state, g_conv_state_bias), ('dp', 'tensor'))  40.7 us
    reduce_sum x8, other arithmetic, causal_conv(): weight[KERNEL - 1 - delay][None, :] * earlier * doc_masks[delay][:, None]  28.8 us
    dot_general x4, matrix products, right_product(): lax.dot_general(left, weight, (((1,), (1,)), ((), ())), preferred_element...  28.5 us
    dot_general x3, matrix products, token_product(): lax.dot_general(left, right, (((0,), (0,)), ((), ())), preferred_element_...  27.5 us
  transfers between devices with their start and end apart: 2, of which 2 were waited for; matrix products, arithmetic and copies ran while one was open for 5% of the time, Pallas kernels for 0%

commit v1 on v0

v1 whole, which is shorter than its diff:
```python
import functools

import jax
import jax.numpy as jnp
from jax import lax
from jax.sharding import PartitionSpec as P

HEAD_DIM = 64
STATE = 128
KERNEL = 4


epsilon = 1e-05
precise = lax.Precision.HIGHEST


def lag_masks(segment_row):
    length = segment_row.shape[0]
    result = [jnp.ones((length,), jnp.float32)]
    for delay in range(1, KERNEL):
        earlier = jnp.concatenate(
            [jnp.full((delay,), -1, jnp.int32), segment_row[: length - delay]]
        )
        result.append((earlier == segment_row).astype(jnp.float32))
    return result


def causal_conv(values, weight, conv_bias, doc_masks):
    length = values.shape[0]
    summed = conv_bias[None, :] + weight[KERNEL - 1][None, :] * values
    for delay in range(1, KERNEL):
        earlier = jnp.concatenate(
            [jnp.zeros((delay, values.shape[1]), jnp.float32), values[: length - delay]], axis=0
        )
        summed = summed + weight[KERNEL - 1 - delay][None, :] * earlier * doc_masks[delay][:, None]
    return jax.nn.silu(summed)


CHUNK = 128


def head_mix(values, states, step_raw, segment_row, step_bias, decay_log, skip_gain):
    length, inner = values.shape
    heads = step_raw.shape[1]
    chunks = length // CHUNK
    step_size = jax.nn.softplus(step_raw + step_bias[None, :])
    decay_rate = -jnp.exp(decay_log)
    places = jnp.arange(CHUNK)
    lower = places[:, None] >= places[None, :]
    drop = (step_size * decay_rate[None, :]).reshape(chunks, CHUNK, heads)
    running = jnp.einsum("ts,csh->cth", lower.astype(jnp.float32), drop, precision=precise)
    segments = segment_row.reshape(chunks, CHUNK)
    last = segments[:, -1]
    before = jnp.concatenate([jnp.full((1,), -1, jnp.int32), last[:-1]])
    allowed = lower[None] & (segments[:, :, None] == segments[:, None, :])
    state_in = states[:, :STATE].astype(jnp.bfloat16).reshape(chunks, CHUNK, STATE)
    state_out = states[:, STATE:].astype(jnp.bfloat16).reshape(chunks, CHUNK, STATE)
    affinity = jnp.einsum("ctn,csn->cts", state_out, state_in, preferred_element_type=jnp.float32)
    running_head = running.transpose(0, 2, 1)
    step_head = step_size.reshape(chunks, CHUNK, heads).transpose(0, 2, 1)
    decays = jnp.exp(
        jnp.where(
            allowed[:, None], running_head[:, :, :, None] - running_head[:, :, None, :], -1e30
        )
    )
    mixing = (decays * affinity[:, None] * step_head[:, :, None, :]).astype(jnp.bfloat16)
    low_head = values.astype(jnp.bfloat16).reshape(chunks, CHUNK, heads, HEAD_DIM)
    near = jnp.einsum("chts,cshp->cthp", mixing, low_head, preferred_element_type=jnp.float32)
    near = near.reshape(chunks, CHUNK, inner)

    spread = (jnp.arange(inner)[None, :] // HEAD_DIM == jnp.arange(heads)[:, None]).astype(
        jnp.float32
    )
    total = running[:, -1, :]
    at_end = (segments == last[:, None]).astype(jnp.float32)
    from_start = (segments == before[:, None]).astype(jnp.float32)
    keep_scale = (
        jnp.exp(total[:, None, :] - running)
        * step_size.reshape(chunks, CHUNK, heads)
        * at_end[:, :, None]
    )
    read_scale = jnp.exp(running) * from_start[:, :, None]
    carry = jnp.exp(total) * (last == before).astype(jnp.float32)[:, None]
    keep_wide = jnp.einsum("cth,hi->cti", keep_scale, spread, precision=lax.Precision.HIGH)
    read_wide = jnp.einsum("cth,hi->cti", read_scale, spread, precision=lax.Precision.HIGH)
    carry_wide = jnp.einsum("ch,hi->ci", carry, spread, precision=precise)
    kept = (values.reshape(chunks, CHUNK, inner) * keep_wide).astype(jnp.bfloat16)
    gained = jnp.einsum("csn,csi->cni", state_in, kept, preferred_element_type=jnp.float32)
    held = jnp.zeros((STATE, inner), jnp.float32)
    entry = []
    for c in range(chunks):
        entry.append(held.astype(jnp.bfloat16))
        held = held * carry_wide[c][None, :] + gained[c]
    entry = jnp.stack(entry)
    far = jnp.einsum("ctn,cni->cti", state_out, entry, preferred_element_type=jnp.float32)
    mixed = (near + far * read_wide).reshape(length, inner)
    return mixed + jnp.repeat(skip_gain, HEAD_DIM)[None, :] * values


def mixer(
    segment_row,
    value_row,
    state_row,
    step_row,
    conv_value,
    conv_value_bias,
    conv_state,
    conv_state_bias,
    step_bias,
    decay_log,
    skip_gain,
):
    doc_masks = lag_masks(segment_row)
    value_conv = causal_conv(value_row, conv_value, conv_value_bias, doc_masks)
    state_conv = causal_conv(state_row, conv_state, conv_state_bias, doc_masks)
    return head_mix(value_conv, state_conv, step_row, segment_row, step_bias, decay_log, skip_gain)


def right_product(left, weight):
    return lax.dot_general(
        left, weight, (((1,), (1,)), ((), ())), preferred_element_type=jnp.float32
    )


def token_product(left, right):
    return lax.dot_general(
        left, right, (((0,), (0,)), ((), ())), preferred_element_type=jnp.float32
    )


def tensor_sum(part):
    count = lax.axis_size("tensor")
    if count == 1:
        return part
    if count == 2:
        return part + lax.ppermute(part, "tensor", [(0, 1), (1, 0)])
    return lax.psum(part, "tensor")


def local(
    hidden,
    segment_ids,
    norm_gain,
    proj_gate,
    proj_value,
    proj_state,
    proj_step,
    conv_value,
    conv_value_bias,
    conv_state,
    conv_state_bias,
    step_bias,
    decay_log,
    skip_gain,
    gate_gain,
    proj_out,
    out_grad,
):
    seq_count, length, width = hidden.shape
    local_inner = proj_gate.shape[1]
    local_heads = proj_step.shape[1]
    state_width = proj_state.shape[1]
    tensor_count = lax.axis_size("tensor")
    inner_total = local_inner * tensor_count
    every = range(seq_count)

    wides = [hidden[s].astype(jnp.float32) for s in every]
    row_scales = [
        lax.rsqrt(jnp.mean(w * w, axis=-1, keepdims=True) + epsilon) for w in wides
    ]
    normeds = [
        (w * r * norm_gain[None, :]).astype(jnp.bfloat16) for w, r in zip(wides, row_scales)
    ]
    params = (
        conv_value,
        conv_value_bias,
        conv_state,
        conv_state_bias,
        step_bias,
        decay_log,
        skip_gain,
    )
    gate_raws, mixed_outs, mixer_backs, gateds, squares = [], [], [], [], []
    for s in every:
        gate_raw = jnp.dot(normeds[s], proj_gate, preferred_element_type=jnp.float32)
        value_raw = jnp.dot(normeds[s], proj_value, preferred_element_type=jnp.float32)
        state_raw = jnp.dot(normeds[s], proj_state, preferred_element_type=jnp.float32)
        step_raw = jnp.dot(normeds[s], proj_step, preferred_element_type=jnp.float32)
        mixed_out, back = jax.vjp(
            jax.checkpoint(functools.partial(mixer, segment_ids[s])),
            value_raw,
            state_raw,
            step_raw,
            *params,
        )
        gated = mixed_out * jax.nn.silu(gate_raw)
        gate_raws.append(gate_raw)
        mixed_outs.append(mixed_out)
        mixer_backs.append(back)
        gateds.append(gated)
        squares.append(jnp.sum(gated * gated, axis=-1))

    d_output_ins = [
        jnp.dot(out_grad[s], proj_out, preferred_element_type=jnp.float32) for s in every
    ]
    inners = [
        jnp.sum(d_output_ins[s] * gate_gain[None, :] * gateds[s], axis=-1) for s in every
    ]
    both = lax.psum(jnp.stack(squares + inners), "tensor")
    block_outs, output_ins, d_gates, d_mixeds = [], [], [], []
    grad_gate_gain = jnp.zeros((local_inner,), jnp.float32)
    for s in every:
        gated, gate_raw = gateds[s], gate_raws[s]
        gated_scale = lax.rsqrt(both[s] / inner_total + epsilon)[:, None]
        gate_inner = both[seq_count + s][:, None]
        output_in = (gated * gated_scale * gate_gain[None, :]).astype(jnp.bfloat16)
        branch = tensor_sum(right_product(output_in, proj_out))
        block_outs.append((wides[s] + branch).astype(jnp.bfloat16))
        d_output_in = d_output_ins[s]
        grad_gate_gain = grad_gate_gain + jnp.sum(d_output_in * gated * gated_scale, axis=0)
        weighted = d_output_in * gate_gain[None, :]
        d_gated = gated_scale * weighted - gated_scale**3 * gated * gate_inner / inner_total
        sigma = jax.nn.sigmoid(gate_raw)
        d_mixeds.append(d_gated * gate_raw * sigma)
        d_gates.append(
            (d_gated * mixed_outs[s] * sigma * (1.0 + gate_raw * (1.0 - sigma))).astype(
                jnp.bfloat16
            )
        )
        output_ins.append(output_in)

    normed_all = jnp.concatenate(normeds, axis=0)
    early = lax.psum_scatter(
        jnp.concatenate(
            [
                token_product(normed_all, jnp.concatenate(d_gates, axis=0)),
                token_product(
                    out_grad.reshape(seq_count * length, width),
                    jnp.concatenate(output_ins, axis=0),
                ),
            ],
            axis=1,
        ),
        "dp",
        scatter_dimension=0,
        tiled=True,
    )

    late_weight = jnp.concatenate([proj_value, proj_state, proj_step], axis=1)
    param_grads, lates, grad_hiddens = None, [], []
    grad_norm_gain = jnp.zeros((width,), jnp.float32)
    for s in every:
        d_value, d_state, d_step, *grads = mixer_backs[s](d_mixeds[s])
        param_grads = grads if s == 0 else [a + b for a, b in zip(param_grads, grads)]
        late = jnp.concatenate([d_value, d_state, d_step], axis=1).astype(jnp.bfloat16)
        lates.append(late)
        part = right_product(d_gates[s], proj_gate) + right_product(late, late_weight)
        row_scale, wide = row_scales[s], wides[s]
        grad_norm_gain = grad_norm_gain + jnp.sum(part * wide * row_scale, axis=0)
        d_scaled = tensor_sum(part) * norm_gain[None, :]
        norm_inner = jnp.sum(d_scaled * wide, axis=-1, keepdims=True)
        grad_hiddens.append(
            out_grad[s].astype(jnp.float32)
            + row_scale * d_scaled
            - row_scale**3 * wide * norm_inner / width
        )
    later = lax.psum_scatter(
        token_product(normed_all, jnp.concatenate(lates, axis=0)),
        "dp",
        scatter_dimension=0,
        tiled=True,
    )
    edge_state = local_inner + state_width
    grad_proj_state = lax.psum(later[:, local_inner:edge_state], "tensor")

    g_cv, g_cvb, g_cs, g_csb, g_sb, g_dl, g_sg = param_grads
    own = [g_cv, g_cvb, g_sb, g_dl, g_sg, grad_gate_gain]
    shared = [g_cs, g_csb, grad_norm_gain]
    own_flat = jnp.concatenate([g.reshape(-1) for g in own])
    place = lax.axis_index("tensor")
    mine = (jnp.arange(tensor_count) == place)[:, None]
    slots = jnp.where(mine, own_flat[None, :], 0.0).reshape(-1)
    packed = lax.psum(
        jnp.concatenate([slots] + [g.reshape(-1) for g in shared]), ("dp", "tensor")
    )
    own_sum = lax.dynamic_slice(packed, (place * own_flat.shape[0],), (own_flat.shape[0],))
    shared_sum = packed[slots.shape[0] :]

    def split(flat, like):
        result, edge = [], 0
        for g in like:
            result.append(flat[edge : edge + g.size].reshape(g.shape))
            edge += g.size
        return result

    r_cv, r_cvb, r_sb, r_dl, r_sg, r_gg = split(own_sum, own)
    r_cs, r_csb, r_ng = split(shared_sum, shared)
    return (
        jnp.stack(block_outs),
        jnp.stack(grad_hiddens),
        r_ng,
        early[:, :local_inner],
        later[:, :local_inner],
        grad_proj_state,
        later[:, edge_state:],
        r_cv,
        r_cvb,
        r_cs,
        r_csb,
        r_sb,
        r_dl,
        r_sg,
        r_gg,
        early[:, local_inner:],
    )


def solution(mesh):
    in_specs = (
        P("dp", None, None),
        P("dp", None),
        P(),
        P(None, "tensor"),
        P(None, "tensor"),
        P(),
        P(None, "tensor"),
        P(None, "tensor"),
        P("tensor"),
        P(),
        P(),
        P("tensor"),
        P("tensor"),
        P("tensor"),
        P("tensor"),
        P(None, "tensor"),
        P("dp", None, None),
    )
    out_specs = (
        P("dp", None, None),
        P("dp", None, None),
        P(),
        P("dp", "tensor"),
        P("dp", "tensor"),
        P("dp", None),
        P("dp", "tensor"),
        P(None, "tensor"),
        P("tensor"),
        P(),
        P(),
        P("tensor"),
        P("tensor"),
        P("tensor"),
        P("tensor"),
        P("dp", "tensor"),
    )
    return jax.shard_map(local, mesh=mesh, in_specs=in_specs, out_specs=out_specs, check_vma=False)
```

time: 1180 us -> 1020 us (0.86)
  waiting for transfers between devices: 415 us -> 268 us
  matrix products: 311 us -> 221 us
  local copies, waits for them, and re-layouts: 115 us -> 155 us
  other arithmetic: 189 us -> 218 us
    psum x1, waiting for transfers between devices: 398 us -> 16.4 us  [local(): grad_proj_state = lax.psum(later[:, local_inner:edge_state], 'tensor')]
    ppermute x0 -> x4, waiting for transfers between devices: none -> 251 us  [tensor_sum(): return part + lax.ppermute(part, 'tensor', [(0, 1), (1, 0)])]
    dot_general x21 -> x64, matrix products: 255 us -> 171 us  [the longest x6 50.3 us: head_mix(): jnp.einsum('chts,cshp->cthp', mixing, low_head, preferred_element_type=jn...]
    unnamed x92 -> x564, local copies, waits for them, and re-layouts: 5.3 us -> 46.6 us
    reshape x0 -> x12, local copies, waits for them, and re-layouts: none -> 39.3 us  [the longest x4 25.6 us: head_mix(): values.astype(jnp.bfloat16).reshape(chunks, CHUNK, heads, HEAD_DIM)]
    reduce_sum x7 -> x14, other arithmetic: 20.7 us -> 59.8 us  [the longest x4 27.6 us: head_mix(): return mixed + jnp.repeat(skip_gain, HEAD_DIM)[None, :] * values]
    another operation x19 -> x11, other arithmetic: 58.4 us -> 29.2 us  [the longest x2 16.5 us: local(): jnp.stack(grad_hiddens)]
    convert_element_type x2 -> x4, local copies, waits for them, and re-layouts: 6.23 us -> 29.5 us  [head_mix(): values.astype(jnp.bfloat16).reshape(chunks, CHUNK, heads, HEAD_DIM)]
  transfers between devices with their start and end apart: 2 -> 7, of which waited for: 2 -> 4; matrix products, arithmetic and copies ran while one was open for 5% -> 9% of each run, Pallas kernels for 0% -> 0%
where the time goes in v1:
time: 1020 us; the launch traced here: 1000 us
  waiting for transfers between devices  268 us (26%)
  matrix products  221 us (22%)
  other arithmetic  218 us (21%)
  local copies, waits for them, and re-layouts  155 us (15%)
  blocking collectives  119 us (12%)
  between operations  17.1 us (2%)
    ppermute x4, waiting for transfers between devices, tensor_sum(): return part + lax.ppermute(part, 'tensor', [(0, 1), (1, 0)])  251 us
    psum x1, blocking collectives, local(): lax.psum(jnp.concatenate([slots] + [g.reshape(-1) for g in shared]), ('dp...  109 us
    dot_general x6, matrix products, head_mix(): jnp.einsum('chts,cshp->cthp', mixing, low_head, preferred_element_type=jn...  50.3 us
    unnamed x564, local copies, waits for them, and re-layouts  46.6 us
    reduce_sum x8, other arithmetic, causal_conv(): weight[KERNEL - 1 - delay][None, :] * earlier * doc_masks[delay][:, None]  29.8 us
    convert_element_type x4, local copies, waits for them, and re-layouts, head_mix(): values.astype(jnp.bfloat16).reshape(chunks, CHUNK, heads, HEAD_DIM)  29.5 us
    reduce_sum x4, other arithmetic, head_mix(): return mixed + jnp.repeat(skip_gain, HEAD_DIM)[None, :] * values  27.6 us
    dot_general x6, matrix products, right_product(): lax.dot_general(left, weight, (((1,), (1,)), ((), ())), preferred_element...  27 us
  transfers between devices with their start and end apart: 7, of which 4 were waited for; matrix products, arithmetic and copies ran while one was open for 9% of the time, Pallas kernels for 0%

profile of v1, /device:TPU:0, one launch (start us, length us, event | category | flops | bytes accessed | tf_op | source)
XLA Modules:
  0.0 1003.3 jit_solution(18028607774672307865)
XLA Ops:
  55.0 21.7 %fusion.446 = (bf16[1024,1024]{1,0:T(8,128)(2,1)}, f32[1024,1024]{1,0:T(8,128)}, bf16[1024,1024]{1,0:T(8,128)(2,1)}, f32[1024,1024]{1,0:T(8,128)S(1)}) fusion(f32[1024]{0:T(1024)S(1)} %get-tuple-element.459, f32[1021,1024]{1,0:T(8,128)} %bitcast.712, f32[1024]{0:T(1024)} %bitcast.949, f32[1024]{0:T(1024)S(1)} %get-tuple-element.458, ...), kind=kLoop, calls=%fused_computation.727 | loop fusion | flops 33554432 | bytes 46133248 | tf_op jit(solution)/shard_map/jvp()/convert_element_type | solution.py:67
  122.2 7.7 fusion.30
  150.3 15.2 %multiply_reduce_fusion.15 = (f32[1024]{0:T(1024)S(1)}, f32[1024]{0:T(1024)S(1)}, f32[1024,1024]{1,0:T(8,128)}, f32[1024]{0:T(1024)S(1)}, f32[1024]{0:T(1024)S(1...) fusion(f32[1024]{0:T(1024)S(1)} %copy-done.246, f32[1024,1024]{1,0:T(8,128)} %fusion.476, ...), kind=kOutput, calls=%fused_computation.180 | convolution fusion | flops 2172645376 | bytes 46161920 | tf_op jit(solution)/shard_map/dot_general | solution.py:204
  165.4 9.7 psum.21
  175.2 21.0 %multiply_multiply_fusion.1 = (f32[1024,1024]{1,0:T(8,128)}, bf16[1024,1024]{1,0:T(8,128)(2,1)}, f32[1024]{0:T(1024)}, bf16[1024,1024]{1,0:T(8,128)(2,1)}, bf16[...) fusion(f32[1024,1024]{1,0:T(8,128)} %fusion.476, ...), kind=kLoop, calls=%fused_computation.163 | loop fusion | flops 54523904 | bytes 58761216 | tf_op jit(solution)/shard_map/mul | solution.py:224
  220.1 13.7 %multiply_reduce_fusion.2 = (f32[1024]{0:T(1024)}, f32[1024,1024]{1,0:T(8,128)S(1)}, f32[1024,1024]{1,0:T(8,128)}) fusion(f32[1024,1024]{1,0:T(8,128)} %get-tuple-element.60, f32[1024]{0:T(1024)S(1)} %copy-done.154, f32[1021,1024]{1,0:T(8,128)} %bitcast.724, f32[1024]{0:T(1024)S(1)} %bitcast.926, f32[1024]{0:T(1024)S(1)} %copy-done.147, ...), kind=kLoop, calls=%fused_computation.124 | loop fusion | flops 17824768 | bytes 29372416 | tf_op jit(solution)/shard_map/transpose(jvp(jvp()))/checkpoint/reduce_sum | solution.py:97
  273.4 13.7 %multiply_reduce_fusion.3 = (f32[1024]{0:T(1024)}, f32[1024,1024]{1,0:T(8,128)S(1)}, f32[1024,1024]{1,0:T(8,128)}) fusion(f32[1024,1024]{1,0:T(8,128)} %get-tuple-element.46, f32[1024]{0:T(1024)S(1)} %copy-done.151, f32[1021,1024]{1,0:T(8,128)} %bitcast.715, f32[1024]{0:T(1024)S(1)} %bitcast.920, f32[1024]{0:T(1024)S(1)} %copy-done.140, ...), kind=kLoop, calls=%fused_computation.125 | loop fusion | flops 17824768 | bytes 29372416 | tf_op jit(solution)/shard_map/transpose(jvp(jvp()))/checkpoint/reduce_sum | solution.py:97
  318.1 7.6 reshape.1880
  325.9 9.8 multiply_reduce_fusion.7
  356.0 11.5 %fusion.17 = (f32[8,16,128]{2,1,0:T(8,128)}, f32[8,16,128]{2,1,0:T(8,128)}, f32[8,16,128]{2,1,0:T(8,128)S(1)}, bf16[8,128,128]{2,1,0:T(8,128)(2,1)S(1)}) fusion(f32[8,16,128]{2,1,0:T(8,128)S(1)} %copy-done.170, f32[8,128,128]{2,1,0:T(8,128)} %fusion.491, f32[8,16,128]{2,1,0:T(8,128)S(1)} %fusion.299, pred[8,128,128]{2,1,0:T(8,128)(4,1)S(1)} %copy-done.117, ...), kind=kOutput, calls=%fused_computation.41 | convolution fusion | flops 297615360 | bytes 5439488 | tf_op jit(solution)/shard_map/transpose(jvp(jvp()))/checkpoint/chts,cshp->cthp/dot_general | solution.py:68
  407.8 7.6 reshape.1878
  415.5 9.9 multiply_reduce_fusion.11
  445.7 11.6 %fusion.15 = (f32[8,16,128]{2,1,0:T(8,128)}, f32[8,16,128]{2,1,0:T(8,128)}, f32[8,16,128]{2,1,0:T(8,128)S(1)}, bf16[8,128,128]{2,1,0:T(8,128)(2,1)S(1)}) fusion(f32[8,16,128]{2,1,0:T(8,128)S(1)} %copy-done.168, f32[8,128,128]{2,1,0:T(8,128)S(1)} %copy-done.96, f32[8,16,128]{2,1,0:T(8,128)S(1)} %fusion.302, pred[8,128,128]{2,1,0:T(8,128)(4,1)S(1)} %copy-done.115, ...), kind=kOutput, calls=%fused_computation.39 | convolution fusion | flops 297615360 | bytes 5439488 | tf_op jit(solution)/shard_map/transpose(jvp(jvp()))/checkpoint/chts,cshp->cthp/dot_general | solution.py:68
  483.7 8.6 fusion.432
  506.0 11.0 %fusion.18 = f32[1024,1296]{1,0:T(8,128)} fusion(bf16[1024,16]{1,0:T(8,128)(2,1)S(1)} %copy-done.104, bf16[1024,256]{1,0:T(8,128)(2,1)S(1)} %copy-done.90, bf16[1024,1024]{1,0:T(8,128)(2,1)S(1)} %get-tuple-element.293, bf16[1024,16]{1,0:T(8,128)(2,1)S(1)} %get-tuple-element.217, bf16[1024,256]{1,0:T(8,128)(2,1)S(1)} %get-tuple-element.306, ...), kind=kOutput, calls=%fused_computation.44 | convolution fusion | flops 5476057088 | bytes 14811136 | tf_op jit(solution)/shard_map/dot_general | solution.py:126
  517.3 8.2 fusion.62
  534.3 9.3 copy.351
  577.1 71.7 %collective-permute-done.3 = f32[1024,1024]{1,0:T(8,128)} collective-permute-done((f32[1024,1024]{1,0:T(8,128)}, f32[1024,1024]{1,0:T(8,128)}, u32[]{:S(2)}, u32[]{:S(2)}) %collective-permute-start.3) | collective-permute-done | bytes 4194336 | tf_op jit(solution)/shard_map/ppermute | solution.py:136
  648.8 89.9 %collective-permute-done.2 = f32[1024,1024]{1,0:T(8,128)} collective-permute-done((f32[1024,1024]{1,0:T(8,128)}, f32[1024,1024]{1,0:T(8,128)}, u32[]{:S(2)}, u32[]{:S(2)}) %collective-permute-start.2) | collective-permute-done | bytes 4194336 | tf_op jit(solution)/shard_map/ppermute | solution.py:136
  738.7 89.9 %collective-permute-done = f32[1024,1024]{1,0:T(8,128)} collective-permute-done((f32[1024,1024]{1,0:T(8,128)}, f32[1024,1024]{1,0:T(8,128)}, u32[]{:S(2)}, u32[]{:S(2)}) %collective-permute-start) | collective-permute-done | bytes 4194336 | tf_op jit(solution)/shard_map/ppermute | solution.py:136
  828.6 12.4 %fusion.50 = (f32[1024]{0:T(1024)S(1)}, f32[1024]{0:T(1024)S(1)}, f32[1024]{0:T(1024)S(1)}, f32[1024]{0:T(1024)S(1)}, bf16[1,1024,1024]{2,1,0:T(8,128)(2,1)}) fusion(f32[1024,1024]{1,0:T(8,128)} %fusion.146, f32[1024]{0:T(1024)S(1)} %copy-done.166, bf16[2,1024,1024]{2,1,0:T(8,128)(2,1)} %param.18, f32[1024]{0:T(1024)S(1)} %copy-done.179, ...), kind=kLoop, calls=%fused_computation.80 | loop fusion | flops 19918848 | bytes 31485952 | tf_op jit(solution)/shard_map/reduce_sum | solution.py:259
  841.0 109.1 %psum.22 = f32[14688]{0:T(1024)S(1)} all-reduce(f32[14688]{0:T(1024)S(1)} %concatenate.226), channel_id=1, replica_groups=mesh['dp'=16,'tensor'=2] {'dp','tensor'}, use_global_device_ids=true, to_apply=%region_65.67 | all-reduce | flops 14688 | bytes 117504 | tf_op jit(solution)/shard_map/psum | solution.py:283
  953.4 12.2 %fusion.47 = (f32[1,1024,1024]{2,1,0:T(8,128)S(1)}, f32[1,1024,1024]{2,1,0:T(8,128)S(1)}, bf16[1,1024,1024]{2,1,0:T(8,128)(2,1)S(1)}) fusion(f32[1024]{0:T(1024)S(1)} %get-tuple-element.155, f32[1024]{0:T(1024)S(1)} %copy-done.212, f32[1024]{0:T(1024)S(1)} %copy-done.166, bf16[2,1024,1024]{2,1,0:T(8,128)(2,1)} %param.34, f32[1024]{0:T(1024)S(1)} %copy-done.179, ...), kind=kLoop, calls=%fused_computation.77 | loop fusion | flops 24117248 | bytes 44068864 | tf_op jit(solution)/shard_map/stack | solution.py:300
  978.7 16.4 %all-reduce.96.cloned.1.call-done = f32[64,256]{1,0:T(8,128)} async-done(((f32[64,256]{1,0:T(8,128)}), f32[64,256]{1,0:T(8,128)}) %all-reduce.96.cloned.1.call-update) | async-done | bytes 65552 | tf_op jit(solution)/shard_map/psum | solution.py:274
  (832 shorter events, 386.9 us)
Async XLA Ops:
  7.2 128.2 %copy-start = (bf16[1024,1024]{1,0:T(8,128)(2,1)S(1)}, bf16[1024,1024]{1,0:T(8,128)(2,1)}, u32[]{:S(2)}) copy-start(bf16[1024,1024]{1,0:T(8,128)(2,1)} %param.33) | copy-start | bytes 6291460
  7.2 965.0 %reduce-scatter.5.cloned.1.call-start = ((), (), s32[]{:S(2)}) async-start(), calls=%async_computation.2 | async-start | bytes 6127616 | tf_op jit(solution)/shard_map/reduce_scatter | solution.py:267
  16.0 19.6 %copy-start.50 = (bf16[1024,1024]{1,0:T(8,128)(2,1)}, bf16[1024,1024]{1,0:T(8,128)(2,1)S(1)}, u32[]{:S(2)}) copy-start(bf16[1024,1024]{1,0:T(8,128)(2,1)S(1)} %get-tuple-element.291) | copy-start | bytes 6291460
  27.2 223.6 %copy-start.4 = (f32[1024,256]{1,0:T(8,128)}, f32[1024,256]{1,0:T(8,128)S(1)}, u32[]{:S(2)}) copy-start(f32[1024,256]{1,0:T(8,128)S(1)} %fusion.472) | copy-start | bytes 3145732
  30.5 60.0 %copy-start.111 = (pred[128,128]{1,0:T(8,128)(4,1)}, pred[128,128]{1,0:T(8,128)(4,1)S(1)}, u32[]{:S(2)}) copy-start(pred[128,128]{1,0:T(8,128)(4,1)S(1)} %iota_compare_fusion.7) | copy-start | bytes 49156
  55.0 21.8 %copy-start.101 = (f32[2,8,8,128]{3,2,1,0:T(8,128)S(1)}, f32[2,8,8,128]{3,2,1,0:T(8,128)}, u32[]{:S(2)}) copy-start(f32[2,8,8,128]{3,2,1,0:T(8,128)} %get-tuple-element.333) | copy-start | bytes 196612
  55.0 21.8 %copy-start.216 = (f32[8,16]{1,0:T(8,128)S(1)}, f32[8,16]{1,0:T(8,128)}, u32[]{:S(2)}) copy-start(f32[8,16]{1,0:T(8,128)} %slice_reduce_fusion.2) | copy-start | bytes 1540
  175.2 22.8 %copy-start.6 = (f32[1024,256]{1,0:T(8,128)S(1)}, f32[1024,256]{1,0:T(8,128)}, u32[]{:S(2)}) copy-start(f32[1024,256]{1,0:T(8,128)} %fusion.479) | copy-start | bytes 3145732
  175.2 22.8 %copy-start.238 = (f32[256]{0:T(256)S(1)}, f32[256]{0:T(256)}, u32[]{:S(2)}) copy-start(f32[256]{0:T(256)} %param.28) | copy-start | bytes 3076
  211.6 27.1 %copy-start.173 = (f32[8,128]{1,0:T(8,128)}, f32[8,128]{1,0:T(8,128)S(1)}, u32[]{:S(2)}) copy-start(f32[8,128]{1,0:T(8,128)S(1)} %get-tuple-element.415) | copy-start | bytes 12292
  216.7 21.9 %copy-start.159 = (f32[8,16]{1,0:T(8,128)}, f32[8,16]{1,0:T(8,128)S(1)}, u32[]{:S(2)}) copy-start(f32[8,16]{1,0:T(8,128)S(1)} %slice_reduce_fusion) | copy-start | bytes 1540
  265.7 26.4 %copy-start.171 = (f32[8,128]{1,0:T(8,128)}, f32[8,128]{1,0:T(8,128)S(1)}, u32[]{:S(2)}) copy-start(f32[8,128]{1,0:T(8,128)S(1)} %get-tuple-element.426) | copy-start | bytes 12292
  271.4 20.8 %copy-start.157 = (f32[8,16]{1,0:T(8,128)}, f32[8,16]{1,0:T(8,128)S(1)}, u32[]{:S(2)}) copy-start(f32[8,16]{1,0:T(8,128)S(1)} %slice_reduce_fusion.1) | copy-start | bytes 1540
  517.0 459.9 %reduce-scatter.7.cloned.1.call-start = ((), (), s32[]{:S(2)}) async-start(), calls=%async_computation.4 | async-start | bytes 8912896
  543.7 451.4 %all-reduce.96.cloned.1.call-start = ((), (), s32[]{:S(2)}) async-start(), calls=%async_computation.3 | async-start | bytes 131072 | tf_op jit(solution)/shard_map/psum | solution.py:274
  554.9 93.8 %collective-permute-start.3 = (f32[1024,1024]{1,0:T(8,128)}, f32[1024,1024]{1,0:T(8,128)}, u32[]{:S(2)}, u32[]{:S(2)}) collective-permute-start(f32[1024,1024]{1,0:T(8,128)} %fusion.143), channel_id=1, source_target_pairs={{0,1},{1,0},{2,3},{3,2},{4,5},{5,4},{6,7},{7,6},{8,9},{9,8},{10,11... | collective-permute-start | bytes 12582920 | tf_op jit(solution)/shard_map/ppermute | solution.py:136
  562.9 175.8 %collective-permute-start.2 = (f32[1024,1024]{1,0:T(8,128)}, f32[1024,1024]{1,0:T(8,128)}, u32[]{:S(2)}, u32[]{:S(2)}) collective-permute-start(f32[1024,1024]{1,0:T(8,128)} %fusion.146), channel_id=1, source_target_pairs={{0,1},{1,0},{2,3},{3,2},{4,5},{5,4},{6,7},{7,6},{8,9},{9,8},{10,11... | collective-permute-start | bytes 12582920 | tf_op jit(solution)/shard_map/ppermute | solution.py:136
  569.6 259.0 %copy-start.164 = (f32[1024]{0:T(1024)S(1)}, f32[1024]{0:T(1024)}, u32[]{:S(2)}) copy-start(f32[1024]{0:T(1024)} %copy-done.163) | copy-start | bytes 12292
  569.6 258.9 %copy-start.166 = (f32[1024]{0:T(1024)S(1)}, f32[1024]{0:T(1024)}, u32[]{:S(2)}) copy-start(f32[1024]{0:T(1024)} %copy-done.165) | copy-start | bytes 12292
  569.6 258.9 %copy-start.179 = (f32[1024]{0:T(1024)S(1)}, f32[1024]{0:T(1024)}, u32[]{:S(2)}) copy-start(f32[1024]{0:T(1024)} %param.20) | copy-start | bytes 12292
  569.6 258.9 %collective-permute-start = (f32[1024,1024]{1,0:T(8,128)}, f32[1024,1024]{1,0:T(8,128)}, u32[]{:S(2)}, u32[]{:S(2)}) collective-permute-start(f32[1024,1024]{1,0:T(8,128)} %fusion.484), channel_id=1, source_target_pairs={{0,1},{1,0},{2,3},{3,2},{4,5},{5,4},{6,7},{7,6},{8,9},{9,8},{10,11... | collective-permute-start | bytes 12582920 | tf_op jit(solution)/shard_map/ppermute | solution.py:136
  574.2 379.1 %collective-permute-start.1 = (f32[1024,1024]{1,0:T(8,128)}, f32[1024,1024]{1,0:T(8,128)}, u32[]{:S(2)}, u32[]{:S(2)}) collective-permute-start(f32[1024,1024]{1,0:T(8,128)} %fusion.485), channel_id=1, source_target_pairs={{0,1},{1,0},{2,3},{3,2},{4,5},{5,4},{6,7},{7,6},{8,9},{9,8},{10,11... | collective-permute-start | bytes 12582920 | tf_op jit(solution)/shard_map/ppermute | solution.py:136
  577.1 376.2 %copy-start.211 = (f32[1024]{0:T(1024)S(1)}, f32[1024]{0:T(1024)}, u32[]{:S(2)}) copy-start(f32[1024]{0:T(1024)} %get-tuple-element.412) | copy-start | bytes 12292
  577.1 376.2 %copy-start.212 = (f32[1024]{0:T(1024)S(1)}, f32[1024]{0:T(1024)}, u32[]{:S(2)}) copy-start(f32[1024]{0:T(1024)} %get-tuple-element.457) | copy-start | bytes 12292
  (256 other events, 1593.2 us)
Sparse Core Ops, SparseCore 0:
  517.1 81.8 reduce-scatter.4
  603.0 103.8 reduce-scatter.6
  975.3 19.7 all-reduce.95

commit v2 on v1

--- a/solution.py
+++ b/solution.py
@@ -128,13 +128,19 @@
     )
 
 
-def tensor_sum(part):
+def tensor_others(part):
     count = lax.axis_size("tensor")
-    if count == 1:
-        return part
     if count == 2:
-        return part + lax.ppermute(part, "tensor", [(0, 1), (1, 0)])
+        return lax.ppermute(part, "tensor", [(0, 1), (1, 0)])
     return lax.psum(part, "tensor")
+
+
+def tensor_join(part, others):
+    return part + others if lax.axis_size("tensor") == 2 else others
+
+
+def after(value, *earlier):
+    return lax.optimization_barrier((value, *earlier))[0]
 
 
 def local(
@@ -207,15 +213,15 @@
         jnp.sum(d_output_ins[s] * gate_gain[None, :] * gateds[s], axis=-1) for s in every
     ]
     both = lax.psum(jnp.stack(squares + inners), "tensor")
-    block_outs, output_ins, d_gates, d_mixeds = [], [], [], []
+    branches, received, output_ins, d_gates, d_mixeds = [], [], [], [], []
     grad_gate_gain = jnp.zeros((local_inner,), jnp.float32)
     for s in every:
         gated, gate_raw = gateds[s], gate_raws[s]
         gated_scale = lax.rsqrt(both[s] / inner_total + epsilon)[:, None]
         gate_inner = both[seq_count + s][:, None]
         output_in = (gated * gated_scale * gate_gain[None, :]).astype(jnp.bfloat16)
-        branch = tensor_sum(right_product(output_in, proj_out))
-        block_outs.append((wides[s] + branch).astype(jnp.bfloat16))
+        branches.append(right_product(output_in, proj_out))
+        received.append(tensor_others(branches[s]))
         d_output_in = d_output_ins[s]
         grad_gate_gain = grad_gate_gain + jnp.sum(d_output_in * gated * gated_scale, axis=0)
         weighted = d_output_in * gate_gain[None, :]
@@ -230,49 +236,35 @@
         output_ins.append(output_in)
 
     normed_all = jnp.concatenate(normeds, axis=0)
-    early = lax.psum_scatter(
-        jnp.concatenate(
-            [
-                token_product(normed_all, jnp.concatenate(d_gates, axis=0)),
-                token_product(
-                    out_grad.reshape(seq_count * length, width),
-                    jnp.concatenate(output_ins, axis=0),
-                ),
-            ],
-            axis=1,
-        ),
-        "dp",
-        scatter_dimension=0,
-        tiled=True,
-    )
+    early_part = jnp.concatenate(
+        [
+            token_product(normed_all, jnp.concatenate(d_gates, axis=0)),
+            token_product(
+                out_grad.reshape(seq_count * length, width),
+                jnp.concatenate(output_ins, axis=0),
+            ),
+        ],
+        axis=1,
+    )
+    early = lax.psum_scatter(early_part, "dp", scatter_dimension=0, tiled=True)
 
     late_weight = jnp.concatenate([proj_value, proj_state, proj_step], axis=1)
-    param_grads, lates, grad_hiddens = None, [], []
+    param_grads, lates, parts, others, grad_hiddens = None, [], [], [], []
+    waits = (early_part, *branches)
     grad_norm_gain = jnp.zeros((width,), jnp.float32)
     for s in every:
-        d_value, d_state, d_step, *grads = mixer_backs[s](d_mixeds[s])
+        d_value, d_state, d_step, *grads = mixer_backs[s](after(d_mixeds[s], *waits))
         param_grads = grads if s == 0 else [a + b for a, b in zip(param_grads, grads)]
         late = jnp.concatenate([d_value, d_state, d_step], axis=1).astype(jnp.bfloat16)
         lates.append(late)
         part = right_product(d_gates[s], proj_gate) + right_product(late, late_weight)
-        row_scale, wide = row_scales[s], wides[s]
-        grad_norm_gain = grad_norm_gain + jnp.sum(part * wide * row_scale, axis=0)
-        d_scaled = tensor_sum(part) * norm_gain[None, :]
-        norm_inner = jnp.sum(d_scaled * wide, axis=-1, keepdims=True)
-        grad_hiddens.append(
-            out_grad[s].astype(jnp.float32)
-            + row_scale * d_scaled
-            - row_scale**3 * wide * norm_inner / width
-        )
-    later = lax.psum_scatter(
-        token_product(normed_all, jnp.concatenate(lates, axis=0)),
-        "dp",
-        scatter_dimension=0,
-        tiled=True,
-    )
+        grad_norm_gain = grad_norm_gain + jnp.sum(part * wides[s] * row_scales[s], axis=0)
+        parts.append(part)
+        if s < seq_count - 1:
+            parts[s] = after(part, received[s])
+            others.append(tensor_others(parts[s]))
+            waits = (part, received[s])
     edge_state = local_inner + state_width
-    grad_proj_state = lax.psum(later[:, local_inner:edge_state], "tensor")
-
     g_cv, g_cvb, g_cs, g_csb, g_sb, g_dl, g_sg = param_grads
     own = [g_cv, g_cvb, g_sb, g_dl, g_sg, grad_gate_gain]
     shared = [g_cs, g_csb, grad_norm_gain]
@@ -281,10 +273,39 @@
     mine = (jnp.arange(tensor_count) == place)[:, None]
     slots = jnp.where(mine, own_flat[None, :], 0.0).reshape(-1)
     packed = lax.psum(
-        jnp.concatenate([slots] + [g.reshape(-1) for g in shared]), ("dp", "tensor")
+        after(
+            jnp.concatenate([slots] + [g.reshape(-1) for g in shared]),
+            early,
+            received[-1],
+            *others,
+        ),
+        ("dp", "tensor"),
     )
     own_sum = lax.dynamic_slice(packed, (place * own_flat.shape[0],), (own_flat.shape[0],))
     shared_sum = packed[slots.shape[0] :]
+
+    later = lax.psum_scatter(
+        token_product(normed_all, after(jnp.concatenate(lates, axis=0), packed)),
+        "dp",
+        scatter_dimension=0,
+        tiled=True,
+    )
+    block_outs = []
+    for s in every:
+        if s == seq_count - 1:
+            parts[s] = after(parts[s], packed)
+            others.append(tensor_others(parts[s]))
+        d_scaled = tensor_join(parts[s], others[s]) * norm_gain[None, :]
+        row_scale, wide = row_scales[s], wides[s]
+        norm_inner = jnp.sum(d_scaled * wide, axis=-1, keepdims=True)
+        grad_hiddens.append(
+            out_grad[s].astype(jnp.float32)
+            + row_scale * d_scaled
+            - row_scale**3 * wide * norm_inner / width
+        )
+        branch = tensor_join(branches[s], received[s])
+        block_outs.append((wide + branch).astype(jnp.bfloat16))
+    grad_proj_state = lax.psum(later[:, local_inner:edge_state], "tensor")
 
     def split(flat, like):
         result, edge = [], 0

time: 1020 us -> 806 us (0.79)
  waiting for transfers between devices: 268 us -> 125 us
  blocking collectives: 119 us -> 50.2 us
  other arithmetic: 218 us -> 237 us
  local copies, waits for them, and re-layouts: 155 us -> 142 us
    ppermute x4, waiting for transfers between devices: 251 us -> 111 us  [tensor_others(): return lax.ppermute(part, 'tensor', [(0, 1), (1, 0)])]
    psum x1, blocking collectives: 109 us -> 40.5 us  [local(): lax.psum(after(jnp.concatenate([slots] + [g.reshape(-1) for g in shared])...]
    concatenate x0 -> x1, other arithmetic: none -> 26.3 us  [local(): jnp.concatenate(lates, axis=0)]
    mul x12, other arithmetic: 24.8 us -> 11.4 us  [causal_conv(): weight[KERNEL - 1 - delay][None, :] * earlier * doc_masks[delay][:, None]]
    dot_general x6, matrix products: 27 us -> 37.4 us  [right_product(): lax.dot_general(left, weight, (((1,), (1,)), ((), ())), preferred_element...]
    unnamed x564 -> x495, local copies, waits for them, and re-layouts: 46.6 us -> 39.8 us
  transfers between devices with their start and end apart: 7 -> 7, of which waited for: 4 -> 3; matrix products, arithmetic and copies ran while one was open for 9% -> 50% of each run, Pallas kernels for 0% -> 0%
where the time goes in v2:
time: 806 us; the launch traced here: 795 us
  other arithmetic  237 us (29%)
  matrix products  220 us (27%)
  local copies, waits for them, and re-layouts  142 us (18%)
  waiting for transfers between devices  125 us (16%)
  blocking collectives  50.2 us (6%)
  between operations  16.9 us (2%)
    ppermute x4, waiting for transfers between devices, tensor_others(): return lax.ppermute(part, 'tensor', [(0, 1), (1, 0)])  111 us
    dot_general x6, matrix products, head_mix(): jnp.einsum('chts,cshp->cthp', mixing, low_head, preferred_element_type=jn...  50.7 us
    psum x1, blocking collectives, local(): lax.psum(after(jnp.concatenate([slots] + [g.reshape(-1) for g in shared])...  40.5 us
    unnamed x495, local copies, waits for them, and re-layouts  39.8 us
    dot_general x6, matrix products, right_product(): lax.dot_general(left, weight, (((1,), (1,)), ((), ())), preferred_element...  37.4 us
    reduce_sum x8, other arithmetic, causal_conv(): weight[KERNEL - 1 - delay][None, :] * earlier * doc_masks[delay][:, None]  30.8 us
    convert_element_type x4, local copies, waits for them, and re-layouts, head_mix(): values.astype(jnp.bfloat16).reshape(chunks, CHUNK, heads, HEAD_DIM)  29.8 us
    reduce_sum x4, other arithmetic, head_mix(): return mixed + jnp.repeat(skip_gain, HEAD_DIM)[None, :] * values  27.3 us
  transfers between devices with their start and end apart: 7, of which 3 were waited for; matrix products, arithmetic and copies ran while one was open for 50% of the time, Pallas kernels for 0%

profile of v2, /device:TPU:0, one launch (start us, length us, event | category | flops | bytes accessed | tf_op | source)
XLA Modules:
  0.0 794.7 jit_solution(9242613608619532424)
XLA Ops:
  50.2 22.6 %fusion.435 = (bf16[1024,1024]{1,0:T(8,128)(2,1)}, f32[1024,1024]{1,0:T(8,128)}, bf16[1024,1024]{1,0:T(8,128)(2,1)}, f32[1024,1024]{1,0:T(8,128)S(1)}) fusion(f32[1024]{0:T(1024)S(1)} %get-tuple-element.468, f32[1021,1024]{1,0:T(8,128)} %bitcast.722, f32[1024]{0:T(1024)S(1)} %bitcast.950, f32[1024]{0:T(1024)S(1)} %get-tuple-element.467, ...), kind=kLoop, calls=%fused_computation.717 | loop fusion | flops 33554432 | bytes 46133248 | tf_op jit(solution)/shard_map/jvp()/convert_element_type | solution.py:67
  116.5 7.6 fusion.18
  144.4 14.7 %multiply_reduce_fusion.15 = (f32[1024]{0:T(1024)S(1)}, f32[1024]{0:T(1024)S(1)}, f32[1024,1024]{1,0:T(8,128)}, f32[1024]{0:T(1024)S(1)}, f32[1024]{0:T(1024)S(1...) fusion(f32[1024]{0:T(1024)S(1)} %copy-done.208, f32[1024,1024]{1,0:T(8,128)} %fusion.465, ...), kind=kOutput, calls=%fused_computation.169 | convolution fusion | flops 2172645376 | bytes 46161920 | tf_op jit(solution)/shard_map/dot_general | solution.py:210
  159.1 9.7 %psum.21 = f32[4,1024]{1,0:T(4,128)S(1)} all-reduce(f32[4,1024]{1,0:T(4,128)S(1)} %pad_maximum_fusion.9), channel_id=1, replica_groups=mesh['dp'=16,'tensor'=2] {'tensor'}, use_global_device_ids=true, to_apply=%region_6.7 | all-reduce | flops 4096 | bytes 32768 | tf_op jit(solution)/shard_map/psum | solution.py:215
  168.9 19.2 %multiply_multiply_fusion.1 = (f32[1024,1024]{1,0:T(8,128)}, bf16[1024,1024]{1,0:T(8,128)(2,1)S(1)}, f32[1024]{0:T(1024)}, bf16[1024,1024]{1,0:T(8,128)(2,1)S(1)...) fusion(f32[1024,1024]{1,0:T(8,128)} %fusion.465, ...), kind=kLoop, calls=%fused_computation.152 | loop fusion | flops 54523904 | bytes 58761216 | tf_op jit(solution)/shard_map/mul | solution.py:230
  208.3 9.2 %copy.351 = f32[1024,2048]{1,0:T(8,128)} copy(f32[1024,2048]{0,1:T(8,128)} %pad_maximum_fusion) | data formatting | bytes 16777216
  248.1 13.2 %multiply_reduce_fusion.3 = (f32[1024]{0:T(1024)}, f32[1024,1024]{1,0:T(8,128)S(1)}, f32[1024,1024]{1,0:T(8,128)}) fusion(f32[1024,1024]{1,0:T(8,128)} %get-tuple-element.53, f32[1024]{0:T(1024)} %copy-done.130, f32[1021,1024]{1,0:T(8,128)} %bitcast.725, f32[1024]{0:T(1024)} %bitcast.927, f32[1024]{0:T(1024)} %copy-done.125, f32[1022,1024]{1,0:T(8,128)} %bitcast.726, ...), kind=kLoop, calls=%fused_computation.115 | loop fusion | flops 17824768 | bytes 29372416 | tf_op jit(solution)/shard_map/transpose(jvp(jvp()))/checkpoint/reduce_sum | solution.py:97
  294.8 7.7 reshape.1878
  305.1 11.4 %multiply_reduce_fusion.11 = (f32[1024]{0:T(1024)}, f32[1024,1024]{1,0:T(8,128)S(1)}, f32[1024,1024]{1,0:T(8,128)}) fusion(f32[1021,1024]{1,0:T(8,128)} %bitcast.728, f32[1024]{0:T(1024)} %copy-done.130, f32[1024,1024]{1,0:T(8,128)} %get-tuple-element.223, f32[1024,1024]{1,0:T(8,128)} %reshape.1878, f32[8,128,1024]{2,1,0:T(8,128)} %get-tuple-element.312, ...), kind=kLoop, calls=%fused_computation.123 | loop fusion | flops 15727616 | bytes 29360128 | tf_op jit(solution)/shard_map/transpose(jvp(jvp()))/checkpoint/reduce_sum | solution.py:35
  325.8 12.3 %fusion.15 = (f32[8,16,128]{2,1,0:T(8,128)}, f32[8,16,128]{2,1,0:T(8,128)}, f32[8,16,128]{2,1,0:T(8,128)S(1)}, bf16[8,128,128]{2,1,0:T(8,128)(2,1)S(1)}) fusion(f32[8,16,128]{2,1,0:T(8,128)} %copy.296, f32[8,128,128]{2,1,0:T(8,128)} %fusion.476, f32[8,16,128]{2,1,0:T(8,128)S(1)} %fusion.291, pred[8,128,128]{2,1,0:T(8,128)(4,1)} %compare_and_fusion.1, ...), kind=kOutput, calls=%fused_computation.39 | convolution fusion | flops 297615360 | bytes 5439488 | tf_op jit(solution)/shard_map/transpose(jvp(jvp()))/checkpoint/chts,cshp->cthp/dot_general | solution.py:68
  385.5 8.5 %fusion.135 = f32[1024,1024]{1,0:T(8,128)} fusion(f32[1024,1024]{1,0:T(8,128)} %fusion.475, bf16[1024,16]{1,0:T(8,128)(2,1)S(1)} %get-tuple-element.227, bf16[1024,256]{1,0:T(8,128)(2,1)S(1)} %get-tuple-element.318, bf16[1024,1024]{1,0:T(8,128)(2,1)S(1)} %get-tuple-element.304, bf16[1024,16]{1,0:T(8,128)(2,1)S(1)} %copy-done.96, ...), kind=kOutput, calls=%fused_computation.223 | convolution fusion | flops 2734882816 | bytes 13697024 | tf_op jit(solution)/shard_map/dot_general | solution.py:120
  421.2 7.6 reshape.1880
  438.3 13.2 %multiply_reduce_fusion.2 = (f32[1024]{0:T(1024)}, f32[1024,1024]{1,0:T(8,128)S(1)}, f32[1024,1024]{1,0:T(8,128)}) fusion(f32[1024,1024]{1,0:T(8,128)} %get-tuple-element.69, f32[1024]{0:T(1024)} %copy-done.128, f32[1021,1024]{1,0:T(8,128)} %bitcast.716, f32[1024]{0:T(1024)} %bitcast.925, f32[1024]{0:T(1024)} %copy-done.120, f32[1022,1024]{1,0:T(8,128)} %bitcast.717, ...), kind=kLoop, calls=%fused_computation.114 | loop fusion | flops 17824768 | bytes 29372416 | tf_op jit(solution)/shard_map/transpose(jvp(jvp()))/checkpoint/reduce_sum | solution.py:97
  461.6 11.3 %fusion.17 = (f32[8,16,128]{2,1,0:T(8,128)}, f32[8,16,128]{2,1,0:T(8,128)}, f32[8,16,128]{2,1,0:T(8,128)S(1)}, bf16[8,128,128]{2,1,0:T(8,128)(2,1)}) fusion(f32[8,16,128]{2,1,0:T(8,128)S(1)} %copy-done.141, f32[8,128,128]{2,1,0:T(8,128)S(1)} %fusion.480, f32[8,16,128]{2,1,0:T(8,128)S(1)} %fusion.288, pred[8,128,128]{2,1,0:T(8,128)(4,1)S(1)} %copy-done.105, ...), kind=kOutput, calls=%fused_computation.41 | convolution fusion | flops 297615360 | bytes 5439488 | tf_op jit(solution)/shard_map/transpose(jvp(jvp()))/checkpoint/chts,cshp->cthp/dot_general | solution.py:68
  500.0 9.2 %multiply_reduce_fusion.7 = (f32[1024]{0:T(1024)S(1)}, f32[1024,1024]{1,0:T(8,128)S(1)}, f32[1024,1024]{1,0:T(8,128)S(1)}) fusion(f32[1021,1024]{1,0:T(8,128)} %bitcast.719, f32[1024]{0:T(1024)S(1)} %copy-done.129, f32[1024,1024]{1,0:T(8,128)} %get-tuple-element.220, f32[1024,1024]{1,0:T(8,128)} %reshape.1880, f32[8,128,1024]{2,1,0:T(8,128)} %get-tuple-element.308, ...), kind=kLoop, calls=%fused_computation.119 | loop fusion | flops 15727616 | bytes 29360128 | tf_op jit(solution)/shard_map/transpose(jvp(jvp()))/checkpoint/reduce_sum | solution.py:35
  526.3 9.6 %fusion.44 = (f32[1024]{0:T(1024)S(1)}, f32[1024]{0:T(1024)S(1)}, f32[1024,1024]{1,0:T(8,128)}) fusion(f32[1024]{0:T(1024)S(1)} %copy-done.152, bf16[2,1024,1024]{2,1,0:T(8,128)(2,1)} %param.18, f32[1024]{0:T(1024)S(1)} %copy-done.154, f32[1024,1024]{1,0:T(8,128)} %fusion.135, f32[1024,1024]{1,0:T(8,128)} %fusion.479, bf16[1024,16]{1,0:T(8,128)(2,1)} %copy.309, ...), kind=kOutput, calls=%fused_computation.75 | convolution fusion | flops 2743269376 | bytes 22102016 | tf_op jit(solution)/shard_map/dot_general | solution.py:120
  536.0 26.3 %maximum_maximum_fusion = bf16[2048,1296]{1,0:T(8,128)(2,1)} fusion(bf16[1024,16]{1,0:T(8,128)(2,1)} %get-tuple-element.225, bf16[1024,256]{1,0:T(8,128)(2,1)S(1)} %get-tuple-element.319, bf16[1024,1024]{1,0:T(8,128)(2,1)} %get-tuple-element.305, bf16[1024,16]{1,0:T(8,128)(2,1)S(1)} %get-tuple-element.227, bf16[1024,256]{1,0:T(8,128)(2,1)S(1)} %copy-done.63, ...), kind=kLoop, calls=%fused_computation.44 | loop fusion | flops 31850496 | bytes 10616832 | tf_op jit(solution)/shard_map/concatenate | solution.py:288
  563.7 25.9 %collective-permute-done.2 = f32[1024,1024]{1,0:T(8,128)} collective-permute-done((f32[1024,1024]{1,0:T(8,128)}, f32[1024,1024]{1,0:T(8,128)}, u32[]{:S(2)}, u32[]{:S(2)}) %collective-permute-start.2) | collective-permute-done | bytes 4194336 | tf_op jit(solution)/shard_map/ppermute | solution.py:134
  589.6 40.5 %psum.22 = f32[14688]{0:T(1024)S(1)} all-reduce(f32[14688]{0:T(1024)S(1)} %concatenate.230), channel_id=1, replica_groups=mesh['dp'=16,'tensor'=2] {'dp','tensor'}, use_global_device_ids=true, to_apply=%region_65.67 | all-reduce | flops 14688 | bytes 117504 | tf_op jit(solution)/shard_map/psum | solution.py:275
  630.2 11.5 %fusion.112 = f32[1024,1296]{1,0:T(8,128)} fusion(bf16[2048,1296]{1,0:T(8,128)(2,1)} %maximum_maximum_fusion, bf16[1024,1024]{1,0:T(8,128)(2,1)} %copy-done.43, bf16[1024,1024]{1,0:T(8,128)(2,1)S(1)} %copy-done.42), kind=kOutput, calls=%fused_computation.204 | convolution fusion | flops 5444206592 | bytes 14811136 | tf_op jit(solution)/shard_map/dot_general | solution.py:126
  649.3 84.6 %collective-permute-done.3 = f32[1024,1024]{1,0:T(8,128)} collective-permute-done((f32[1024,1024]{1,0:T(8,128)}, f32[1024,1024]{1,0:T(8,128)}, u32[]{:S(2)}, u32[]{:S(2)}) %collective-permute-start.3) | collective-permute-done | bytes 4194336 | tf_op jit(solution)/shard_map/ppermute | solution.py:134
  734.0 11.7 %fusion.36 = (f32[1024]{0:T(1024)S(1)}, f32[1024]{0:T(1024)S(1)}, bf16[1,1024,1024]{2,1,0:T(8,128)(2,1)}) fusion(f32[1024]{0:T(1024)S(1)} %copy-done.148, f32[1024,1024]{1,0:T(8,128)} %fusion.135, f32[1024,1024]{1,0:T(8,128)} %collective-permute-done.2, bf16[2,1024,1024]{2,1,0:T(8,128)(2,1)} %param.18, f32[1024,1024]{1,0:T(8,128)} %get-tuple-element.82, ...), kind=kLoop, calls=%fused_computation.67 | loop fusion | flops 13629440 | bytes 31469568 | tf_op jit(solution)/shard_map/reduce_sum | solution.py:300
  745.8 11.8 %fusion.35 = (f32[1,1024,1024]{2,1,0:T(8,128)S(1)}, f32[1,1024,1024]{2,1,0:T(8,128)}, bf16[1,1024,1024]{2,1,0:T(8,128)(2,1)}) fusion(f32[1024]{0:T(1024)S(1)} %get-tuple-element.178, f32[1024]{0:T(1024)S(1)} %copy-done.176, f32[1024]{0:T(1024)S(1)} %copy-done.154, bf16[2,1024,1024]{2,1,0:T(8,128)(2,1)} %param.34, f32[1024]{0:T(1024)S(1)} %copy-done.148, ...), kind=kLoop, calls=%fused_computation.66 | loop fusion | flops 24117248 | bytes 44068864 | tf_op jit(solution)/shard_map/stack | solution.py:321
  772.1 14.4 %all-reduce.96.cloned.1.call-done = f32[64,256]{1,0:T(8,128)} async-done(((f32[64,256]{1,0:T(8,128)}), f32[64,256]{1,0:T(8,128)}) %all-reduce.96.cloned.1.call-update) | async-done | bytes 65552 | tf_op jit(solution)/shard_map/psum | solution.py:308
  (766 shorter events, 364.0 us)
Async XLA Ops:
  7.2 122.4 %copy-start = (bf16[1024,1024]{1,0:T(8,128)(2,1)S(1)}, bf16[1024,1024]{1,0:T(8,128)(2,1)}, u32[]{:S(2)}) copy-start(bf16[1024,1024]{1,0:T(8,128)(2,1)} %param.33) | copy-start | bytes 6291460
  7.2 555.1 %reduce-scatter.7.cloned.1.call-start = ((), (), s32[]{:S(2)}) async-start(), calls=%async_computation.4 | async-start | bytes 8912896
  8.1 77.9 %copy-start.72 = (s32[1,1024]{1,0:T(1,128)}, s32[1,1024]{1,0:T(1,128)S(1)}, u32[]{:S(2)}) copy-start(s32[1,1024]{1,0:T(1,128)S(1)} %get-tuple-element.415) | copy-start | bytes 12292
  16.0 14.7 %copy-start.40 = (bf16[1024,1024]{1,0:T(8,128)(2,1)}, bf16[1024,1024]{1,0:T(8,128)(2,1)S(1)}, u32[]{:S(2)}) copy-start(bf16[1024,1024]{1,0:T(8,128)(2,1)S(1)} %get-tuple-element.300) | copy-start | bytes 6291460
  16.0 19.0 %copy-start.43 = (bf16[1024,1024]{1,0:T(8,128)(2,1)}, bf16[1024,1024]{1,0:T(8,128)(2,1)S(1)}, u32[]{:S(2)}) copy-start(bf16[1024,1024]{1,0:T(8,128)(2,1)S(1)} %get-tuple-element.301) | copy-start | bytes 6291460
  26.3 13.8 %copy-start.75 = (f32[1024,16]{0,1:T(8,128)}, f32[1024,16]{0,1:T(8,128)S(1)}, u32[]{:S(2)}) copy-start(f32[1024,16]{0,1:T(8,128)S(1)} %fusion.467) | copy-start | bytes 196612
  28.9 12.8 %copy-start.5 = (f32[1024,256]{1,0:T(8,128)}, f32[1024,256]{1,0:T(8,128)S(1)}, u32[]{:S(2)}) copy-start(f32[1024,256]{1,0:T(8,128)S(1)} %fusion.468) | copy-start | bytes 3145732
  29.9 195.1 %copy-start.94 = (pred[128,128]{1,0:T(8,128)(4,1)}, pred[128,128]{1,0:T(8,128)(4,1)S(1)}, u32[]{:S(2)}) copy-start(pred[128,128]{1,0:T(8,128)(4,1)S(1)} %iota_compare_fusion.7) | copy-start | bytes 49156
  50.2 22.6 %copy-start.179 = (f32[8,16]{1,0:T(8,128)S(1)}, f32[8,16]{1,0:T(8,128)}, u32[]{:S(2)}) copy-start(f32[8,16]{1,0:T(8,128)} %copy-done.178) | copy-start | bytes 1540
  192.6 201.4 %collective-permute-start = (f32[1024,1024]{1,0:T(8,128)}, f32[1024,1024]{1,0:T(8,128)}, u32[]{:S(2)}, u32[]{:S(2)}) collective-permute-start(f32[1024,1024]{1,0:T(8,128)} %fusion.473), channel_id=1, source_target_pairs={{0,1},{1,0},{2,3},{3,2},{4,5},{5,4},{6,7},{7,6},{8,9},{9,8},{10,11... | collective-permute-start | bytes 12582920 | tf_op jit(solution)/shard_map/ppermute | solution.py:134
  217.6 546.8 %reduce-scatter.5.cloned.1.call-start = ((), (), s32[]{:S(2)}) async-start(), calls=%async_computation.2 | async-start | bytes 6127616 | tf_op jit(solution)/shard_map/reduce_scatter | solution.py:287
  223.7 340.0 %collective-permute-start.1 = (f32[1024,1024]{1,0:T(8,128)}, f32[1024,1024]{1,0:T(8,128)}, u32[]{:S(2)}, u32[]{:S(2)}) collective-permute-start(f32[1024,1024]{1,0:T(8,128)} %fusion.474), channel_id=1, source_target_pairs={{0,1},{1,0},{2,3},{3,2},{4,5},{5,4},{6,7},{7,6},{8,9},{9,8},{10,11... | collective-permute-start | bytes 12582920 | tf_op jit(solution)/shard_map/ppermute | solution.py:134
  363.7 21.7 %copy-start.62 = (bf16[1024,256]{1,0:T(8,128)(2,1)}, bf16[1024,256]{1,0:T(8,128)(2,1)S(1)}, u32[]{:S(2)}) copy-start(bf16[1024,256]{1,0:T(8,128)(2,1)S(1)} %get-tuple-element.318) | copy-start | bytes 1572868
  499.2 90.4 %collective-permute-start.2 = (f32[1024,1024]{1,0:T(8,128)}, f32[1024,1024]{1,0:T(8,128)}, u32[]{:S(2)}, u32[]{:S(2)}) collective-permute-start(f32[1024,1024]{1,0:T(8,128)} %fusion.135), channel_id=1, source_target_pairs={{0,1},{1,0},{2,3},{3,2},{4,5},{5,4},{6,7},{7,6},{8,9},{9,8},{10,11... | collective-permute-start | bytes 12582920 | tf_op jit(solution)/shard_map/ppermute | solution.py:134
  536.0 94.1 %copy-start.42 = (bf16[1024,1024]{1,0:T(8,128)(2,1)S(1)}, bf16[1024,1024]{1,0:T(8,128)(2,1)}, u32[]{:S(2)}) copy-start(bf16[1024,1024]{1,0:T(8,128)(2,1)} %copy-done.40) | copy-start | bytes 6291460
  641.7 92.3 %copy-start.148 = (f32[1024]{0:T(1024)S(1)}, f32[1024]{0:T(1024)}, u32[]{:S(2)}) copy-start(f32[1024]{0:T(1024)} %param.20) | copy-start | bytes 12292
  641.7 144.8 %all-reduce.96.cloned.1.call-start = ((), (), s32[]{:S(2)}) async-start(), calls=%async_computation.3 | async-start | bytes 131072 | tf_op jit(solution)/shard_map/psum | solution.py:308
  642.0 92.0 %collective-permute-start.3 = (f32[1024,1024]{1,0:T(8,128)}, f32[1024,1024]{1,0:T(8,128)}, u32[]{:S(2)}, u32[]{:S(2)}) collective-permute-start(f32[1024,1024]{1,0:T(8,128)} %get-tuple-element.82), channel_id=1, source_target_pairs={{0,1},{1,0},{2,3},{3,2},{4,5},{5,4},{6,7},{7,6},{8,9},{9,8},{10,11... | collective-permute-start | bytes 12582920 | tf_op jit(solution)/shard_map/ppermute | solution.py:134
  649.3 96.4 %copy-start.9 = (bf16[2,1024,1024]{2,1,0:T(8,128)(2,1)S(1)}, bf16[2,1024,1024]{2,1,0:T(8,128)(2,1)}, u32[]{:S(2)}) copy-start(bf16[2,1024,1024]{2,1,0:T(8,128)(2,1)} %param.18) | copy-start | bytes 12582916
  649.3 96.4 %copy-start.25 = (f32[1024,1024]{1,0:T(8,128)S(1)}, f32[1024,1024]{1,0:T(8,128)}, u32[]{:S(2)}) copy-start(f32[1024,1024]{1,0:T(8,128)} %fusion.135) | copy-start | bytes 12582916
  649.3 96.4 %copy-start.26 = (f32[1024,1024]{1,0:T(8,128)S(1)}, f32[1024,1024]{1,0:T(8,128)}, u32[]{:S(2)}) copy-start(f32[1024,1024]{1,0:T(8,128)} %get-tuple-element.82) | copy-start | bytes 12582916
  649.3 96.4 %copy-start.175 = (f32[1024]{0:T(1024)S(1)}, f32[1024]{0:T(1024)}, u32[]{:S(2)}) copy-start(f32[1024]{0:T(1024)} %get-tuple-element.420) | copy-start | bytes 12292
  649.3 96.4 %copy-start.176 = (f32[1024]{0:T(1024)S(1)}, f32[1024]{0:T(1024)}, u32[]{:S(2)}) copy-start(f32[1024]{0:T(1024)} %get-tuple-element.466) | copy-start | bytes 12292
  765.9 22.1 %copy-start.1 = (bf16[1024,1024]{1,0:T(8,128)(2,1)S(1)}, bf16[1024,1024]{1,0:T(8,128)(2,1)}, u32[]{:S(2)}) copy-start(bf16[1024,1024]{1,0:T(8,128)(2,1)} %param.33) | copy-start | bytes 6291460
  (221 other events, 936.8 us)
Sparse Core Ops, SparseCore 0:
  217.7 105.6 reduce-scatter.6
  641.8 81.9 reduce-scatter.4
  766.0 20.4 all-reduce.95
